TPU v7x, 32 devices: a whole 2x2x4 slice. The times are simulated.
32 devices in a mesh: grp: 4 (over z), blk: 8 (over y, x, core).
Axes of the slice: x: 2, y: 2, z: 4, core: 2. Of those that a mesh axis runs over, the one named last changes fastest.
Arguments:
- state: float32 [8, 8, 8, 8, 16384], P(None, None, None, None, ('grp', 'blk')), may hold values from -6 to 6
- counts: int32 [32], P(('grp', 'blk')), may hold values from 384 to 512, as said below
- neighbours: int32 [6, 16384], P(None, ('grp', 'blk')), may hold values from -1 to 16383, as said below
- rows: int32 [16384], P(('grp', 'blk')), may hold values from -1 to 24575, as said below
- rates: float32 [8], replicated, may hold values from 0.02 to 0.16
- conductance: float32 [96, 256], P('blk'), may hold values from 0.5 to 4
Outputs:
- new_state: float32 [8, 8, 8, 8, 16384], P(None, None, None, None, ('grp', 'blk'))
- potential: float32 [96, 256], P('blk')
Inputs may be any that keep to these rules, and one draw needn't show every extreme that they name: `counts`: device 0 has exactly 512 live blocks; live blocks are the first ones of a device's slots. `neighbours`: padded slots name -1 on every face. A live block of device d names a live block of d itself, of d - 1 among its last 128 live blocks, of d + 1 among its first 128 blocks, or -1. `rows`: padded slots have -1; several blocks may name one cell.
All inputs are finite; a program needn't handle non-finite values.
Results may differ from a plain program's by a relative error of at most 0.0001.
Values sent between devices are 32-bit elements; how exact they have to be, the bound alone decides.
A program may use at most 256 MiB of HBM per device.

v0:
```python
import jax
import jax.numpy as jnp
from jax import lax
from jax.sharding import PartitionSpec as P

STEPS = 2
ITERS = 3


def with_halo(cells, sides, width):
    for axis, dim in sides:
        count = lax.axis_size(axis)
        ends = count - 1
        head = lax.slice_in_dim(cells, 0, width, axis=dim)
        tail = lax.slice_in_dim(cells, cells.shape[dim] - width, cells.shape[dim], axis=dim)
        cells = jnp.concatenate(
            [
                lax.ppermute(tail, axis, [(i, (i + 1) % count) for i in range(ends)]),
                cells,
                lax.ppermute(head, axis, [((i + 1) % count, i) for i in range(ends)]),
            ],
            axis=dim,
        )
    return cells


def planes(u):
    return jnp.stack([u[:, 0], u[:, -1], u[:, :, 0], u[:, :, -1], u[:, :, :, 0], u[:, :, :, -1]])


def ghost_planes(table, index, valid, own):
    width = table.shape[-1]
    plane_shape = own.shape[1:]
    flat = table.reshape(6, -1, width)
    columns = jnp.arange(width, dtype=jnp.int32)
    result = []
    for face in range(6):
        selector = (columns[:, None] == index[face][None, :]).astype(jnp.float32)
        taken = jnp.dot(
            flat[face ^ 1],
            selector,
            precision=lax.Precision.HIGHEST,
            preferred_element_type=jnp.float32,
        ).reshape(plane_shape)
        result.append(jnp.where(valid[face], taken, own[face]))
    return result


def stencil(u, ghosts, live, rates):
    lap = -6.0 * u
    lap = (
        lap
        + jnp.concatenate([u[:, 1:], ghosts[1][:, None]], 1)
        + jnp.concatenate([ghosts[0][:, None], u[:, :-1]], 1)
    )
    lap = (
        lap
        + jnp.concatenate([u[:, :, 1:], ghosts[3][:, :, None]], 2)
        + jnp.concatenate([ghosts[2][:, :, None], u[:, :, :-1]], 2)
    )
    lap = (
        lap
        + jnp.concatenate([u[:, :, :, 1:], ghosts[5][:, :, :, None]], 3)
        + jnp.concatenate([ghosts[4][:, :, :, None], u[:, :, :, :-1]], 3)
    )
    return u + rates[:, None, None, None, None] * live[None, None, None, None, :] * lap


def operate(field, conductance):
    padded = with_halo(field, (("blk", 0),), 1)
    beside = padded[2:] + padded[:-2] + jnp.roll(field, 1, 1) + jnp.roll(field, -1, 1)
    return (4.0 + conductance) * field - beside


def squares(residual):
    return lax.psum(jnp.sum(residual * residual), "blk")


def on_device(state, counts, neighbours, rows, rates, conductance):
    slots_dev = state.shape[-1]
    device = lax.axis_index("grp") * lax.axis_size("blk") + lax.axis_index("blk")
    count = counts[0]
    live = (jnp.arange(slots_dev, dtype=jnp.int32) < count).astype(jnp.float32)
    valid = neighbours >= 0
    owner = jnp.where(valid, neighbours, device * slots_dev) // slots_dev
    inside = jnp.where(valid, neighbours, device * slots_dev) - owner * slots_dev
    u = state
    for step in range(STEPS):
        own = planes(u)
        table = with_halo(own, ((("grp", "blk"), 4),), slots_dev)
        index = inside + (owner - device + 1) * slots_dev
        index = jnp.where(valid, index, -1)
        u = stencil(u, ghost_planes(table, index, valid, own), live, rates)
    current = jnp.sum(u[6, 0] - u[5, 0], axis=(0, 1)) / 8.0
    coupled = rows >= 0
    safe = jnp.where(coupled, rows, 0)
    lat_rows, lon_cells = conductance.shape
    blk_count = lax.axis_size("blk")
    cells_dev = lat_rows * lon_cells
    cells = cells_dev * blk_count
    scattered = jnp.zeros((cells,), jnp.float32).at[safe].add(jnp.where(coupled, current, 0.0))
    summed = lax.psum(scattered, "grp")
    share = lax.psum_scatter(summed, "blk", scatter_dimension=0, tiled=True)
    source = share.reshape(lat_rows, lon_cells)
    potential = jnp.zeros_like(source)
    residual = source
    direction = source
    norm_now = squares(residual)
    for step in range(ITERS):
        image = operate(direction, conductance)
        alpha = norm_now / lax.psum(jnp.sum(direction * image), "blk")
        potential = potential + alpha * direction
        residual = residual - alpha * image
        norm_next = squares(residual)
        direction = residual + norm_next / norm_now * direction
        norm_now = norm_next
    whole = lax.all_gather(potential, "blk", axis=0, tiled=True).reshape(-1)
    added = jnp.where(coupled, whole[safe], 0.0)
    u = u.at[1, 0].add(added[None, None, :])
    return (u, potential)


def solution(mesh):
    placed = (
        P(None, None, None, None, ("grp", "blk")),
        P(("grp", "blk")),
        P(None, ("grp", "blk")),
        P(("grp", "blk")),
        P(),
        P("blk", None),
    )
    return jax.shard_map(
        on_device,
        mesh=mesh,
        in_specs=placed,
        out_specs=(P(None, None, None, None, ("grp", "blk")), P("blk", None)),
        check_vma=False,
    )
```

profile of v0, /device:TPU:0, one launch (start us, length us, event | category | flops | bytes accessed | tf_op | source)
XLA Modules:
  0.0 664.3 jit_solution(15600385909471027689)
XLA Ops:
  10.8 8.6 %copy.111 = f32[8,8,8,8,512]{4,2,1,0,3:T(8,128)S(1)} copy(f32[8,8,8,8,512]{4,3,2,1,0:T(8,128)} %param.8) | data formatting | bytes 16777216 | tf_op args[0]
  36.2 13.4 %collective-permute-start.1 = (f32[6,8,8,8,512]{4,3,2,1,0:T(8,128)}, f32[6,8,8,8,512]{4,3,2,1,0:T(8,128)}, u32[]{:S(2)}, u32[]{:S(2)}) collective-permute-start(f32[6,8,8,8,512]{4,3,2,1,0:T(8,128)} %bitcast_dynamic-update-slice_fusion.2), channel_id=1, source_target_pairs={{1,0},{2,1},{3,2},{4,3},{5,4},{6,5},{7,6},{8,7},{9,8},{10,9},{11,1... | collective-permute-start | bytes 18874376 | tf_op jit(solution)/shard_map/ppermute | solution.py:20
  50.5 13.8 %fusion.113 = (f32[8,8,8,7,512]{4,2,1,0,3:T(8,128)}, f32[8,8,8,7,512]{4,2,1,0,3:T(8,128)}) fusion(f32[8,8,8,8,512]{4,2,1,0,3:T(8,128)} %copy-done.1), kind=kLoop, calls=%fused_computation.173 | loop fusion | bytes 29360128 | tf_op jit(solution)/shard_map/slice | solution.py:64
  64.3 12.8 %fusion.115 = (f32[8,7,8,8,512]{4,2,1,0,3:T(8,128)}, f32[8,7,8,8,512]{4,2,1,0,3:T(8,128)}) fusion(f32[8,8,8,8,512]{4,2,1,0,3:T(8,128)} %copy-done.1), kind=kLoop, calls=%fused_computation.175 | loop fusion | bytes 29360128 | tf_op jit(solution)/shard_map/slice | solution.py:54
  77.1 13.4 %fusion.114 = (f32[8,8,7,8,512]{4,2,1,0,3:T(8,128)}, f32[8,8,7,8,512]{4,2,1,0,3:T(8,128)}) fusion(f32[8,8,8,8,512]{4,2,1,0,3:T(8,128)} %copy-done.1), kind=kLoop, calls=%fused_computation.174 | loop fusion | bytes 29360128 | tf_op jit(solution)/shard_map/slice | solution.py:59
  90.5 7.9 %pad_maximum_fusion = f32[6,8,8,8,1536]{4,3,2,1,0:T(8,128)S(1)} fusion(f32[6,8,8,8,512]{4,3,2,1,0:T(8,128)} %collective-permute-done.1, f32[6,8,8,8,512]{4,3,2,1,0:T(8,128)} %bitcast_dynamic-update-slice_fusion.2, f32[6,8,8,8,512]{4,3,2,1,0:T(8,128)} %collective-permute-done), kind=kLoop, calls=%fused_computation.2 | loop fusion | flops 9437184 | bytes 37748736 | tf_op jit(solution)/shard_map/concatenate | solution.py:16
  114.7 6.1 fusion.59
  120.8 6.1 fusion.65
  130.2 18.4 %fusion.6 = f32[8,8,8,8,512]{4,2,1,0,3:T(8,128)S(1)} fusion(f32[8,1,8,8,512]{4,2,1,0,3:T(8,128)} %get-tuple-element.81, f32[8,7,8,8,512]{4,2,1,0,3:T(8,128)} %get-tuple-element.51, f32[8,7,8,8,512]{4,2,1,0,3:T(8,128)} %get-tuple-element.50, f32[8,1,8,8,512]{4,2,1,0,3:T(8,128)S(1)} %get-tuple-element.80, f32[8,8,1,8,512]{4,2,1,0,3:T(1,128)S(1)} %copy.105, ...), kind=kLoop, calls=%fused_computation.11 | loop fusion | flops 31457280 | bytes 67125248 | tf_op jit(solution)/shard_map/add | solution.py:66
  165.4 87.4 %collective-permute-start.2 = (f32[6,8,8,8,512]{4,3,2,1,0:T(8,128)}, f32[6,8,8,8,512]{4,3,2,1,0:T(8,128)}, u32[]{:S(2)}, u32[]{:S(2)}) collective-permute-start(f32[6,8,8,8,512]{4,3,2,1,0:T(8,128)} %bitcast_dynamic-update-slice_fusion), channel_id=1, source_target_pairs={{0,1},{1,2},{2,3},{3,4},{4,5},{5,6},{6,7},{7,8},{8,9},{9,10},{10,1... | collective-permute-start | bytes 18874376 | tf_op jit(solution)/shard_map/ppermute | solution.py:18
  254.1 13.8 %fusion.109 = (f32[8,8,8,7,512]{4,2,1,0,3:T(8,128)}, f32[8,8,8,7,512]{4,2,1,0,3:T(8,128)}) fusion(f32[8,8,8,8,512]{4,2,1,0,3:T(8,128)} %copy-done), kind=kLoop, calls=%fused_computation.169 | loop fusion | bytes 29360128 | tf_op jit(solution)/shard_map/slice | solution.py:64
  267.9 12.8 %fusion.111 = (f32[8,7,8,8,512]{4,2,1,0,3:T(8,128)}, f32[8,7,8,8,512]{4,2,1,0,3:T(8,128)}) fusion(f32[8,8,8,8,512]{4,2,1,0,3:T(8,128)} %copy-done), kind=kLoop, calls=%fused_computation.171 | loop fusion | bytes 29360128 | tf_op jit(solution)/shard_map/slice | solution.py:54
  280.7 13.4 %fusion.110 = (f32[8,8,7,8,512]{4,2,1,0,3:T(8,128)}, f32[8,8,7,8,512]{4,2,1,0,3:T(8,128)}) fusion(f32[8,8,8,8,512]{4,2,1,0,3:T(8,128)} %copy-done), kind=kLoop, calls=%fused_computation.170 | loop fusion | bytes 29360128 | tf_op jit(solution)/shard_map/slice | solution.py:59
  294.2 14.3 %pad_maximum_fusion.1 = f32[6,8,8,8,1536]{4,3,2,1,0:T(8,128)} fusion(f32[6,8,8,8,512]{4,3,2,1,0:T(8,128)} %collective-permute-done.3, f32[6,8,8,8,512]{4,3,2,1,0:T(8,128)} %bitcast_dynamic-update-slice_fusion, f32[6,8,8,8,512]{4,3,2,1,0:T(8,128)} %collective-permute-done.2), kind=kLoop, calls=%fused_computation.3 | loop fusion | flops 9437184 | bytes 37748736 | tf_op jit(solution)/shard_map/concatenate | solution.py:16
  343.5 17.2 %fusion.13 = f32[8,8,8,8,512]{4,2,1,0,3:T(8,128)S(1)} fusion(f32[8,8,8,8,512]{4,2,1,0,3:T(8,128)S(1)} %bitcast.221, f32[8,1,8,8,512]{4,2,1,0,3:T(8,128)S(1)} %get-tuple-element.39, f32[8,7,8,8,512]{4,2,1,0,3:T(8,128)} %get-tuple-element.41, f32[8,7,8,8,512]{4,2,1,0,3:T(8,128)} %get-tuple-element.40, f32[8,1,8,8,512]{4,2,1,0,3:T(8,128)S(1)} %get-tuple-element.38, ...), kind=kLoop, calls=%fused_computation.19 | loop fusion | flops 31457280 | bytes 67125248 | tf_op jit(solution)/shard_map/add | solution.py:66
  370.2 142.2 %all-reduce.4.cloned.1.call-done = f32[24576]{0:T(1024)} async-done(((f32[24576]{0:T(1024)}), f32[24576]{0:T(1024)}) %all-reduce.4.cloned.1.call-update) | async-done | bytes 98320
  513.1 18.7 %psum.56 = f32[3072]{0:T(1024)S(1)} all-reduce(f32[3072]{0:T(1024)S(1)} %dynamic-slice.9), channel_id=1, replica_groups=mesh['grp'=4,'blk'=8] {'grp'}, use_global_device_ids=true, to_apply=%region_2.3 | all-reduce | flops 3072 | bytes 24576 | tf_op jit(solution)/shard_map/psum | solution.py:102
  537.7 14.6 %all-reduce.1 = (f32[]{:T(128)}, f32[]{:T(128)}) all-reduce(f32[]{:T(128)} %multiply_reduce_fusion.4, f32[]{:T(128)} %get-tuple-element.32), channel_id=1, replica_groups=mesh['grp'=4,'blk'=8] {'blk'}, use_global_device_ids=true, to_apply=%region_5.6 | all-reduce | flops 2 | bytes 16 | tf_op jit(solution)/shard_map/psum | solution.py:76
  554.2 12.9 %psum.52 = f32[]{:T(128)} all-reduce(f32[]{:T(128)} %get-tuple-element.30), channel_id=1, replica_groups=mesh['grp'=4,'blk'=8] {'blk'}, use_global_device_ids=true, to_apply=%region_9.10 | all-reduce | flops 1 | bytes 8 | tf_op jit(solution)/shard_map/psum | solution.py:76
  574.3 15.0 %psum.53 = f32[]{:T(128)} all-reduce(f32[]{:T(128)} %get-tuple-element.28), channel_id=1, replica_groups=mesh['grp'=4,'blk'=8] {'blk'}, use_global_device_ids=true, to_apply=%region_11.12 | all-reduce | flops 1 | bytes 8 | tf_op jit(solution)/shard_map/psum | solution.py:111
  591.3 12.6 %psum.54 = f32[]{:T(128)} all-reduce(f32[]{:T(128)} %multiply_reduce_fusion), channel_id=1, replica_groups=mesh['grp'=4,'blk'=8] {'blk'}, use_global_device_ids=true, to_apply=%region_13.14 | all-reduce | flops 1 | bytes 8 | tf_op jit(solution)/shard_map/psum | solution.py:76
  611.2 14.9 %psum.55 = f32[]{:T(128)} all-reduce(f32[]{:T(128)} %fusion.96), channel_id=1, replica_groups=mesh['grp'=4,'blk'=8] {'blk'}, use_global_device_ids=true, to_apply=%region_15.16 | all-reduce | flops 1 | bytes 8 | tf_op jit(solution)/shard_map/psum | solution.py:111
  627.4 10.0 %all-gather = f32[8,12,256]{2,1,0:T(8,128)S(1)} all-gather(f32[1,12,256]{2,1,0:T(8,128)S(1)} %bitcast.230), channel_id=1, replica_groups=mesh['grp'=4,'blk'=8] {'blk'}, dimensions={0}, use_global_device_ids=true | all-gather | bytes 110592 | tf_op jit(solution)/shard_map/all_gather | solution.py:117
  642.3 14.9 %copy.124 = f32[8,8,8,8,512]{4,3,2,1,0:T(8,128)} copy(f32[8,8,8,8,512]{4,2,1,0,3:T(8,128)} %fusion.87) | data formatting | bytes 16777216
  (131 shorter events, 126.3 us)
Async XLA Ops:
  7.2 505.2 %all-reduce.4.cloned.1.call-start = ((), (), s32[]{:S(2)}) async-start(), calls=%async_computation | async-start | bytes 196608
  10.8 12.1 %copy-start.5 = (f32[8,8,1,8,512]{4,3,2,1,0:T(8,128)}, f32[8,8,1,8,512]{4,3,2,1,0:T(8,128)S(1)}, u32[]{:S(2)}) copy-start(f32[8,8,1,8,512]{4,3,2,1,0:T(8,128)S(1)} %get-tuple-element.53) | copy-start | bytes 3145732
  19.5 10.6 %copy-start.1 = (f32[8,8,8,8,512]{4,2,1,0,3:T(8,128)}, f32[8,8,8,8,512]{4,2,1,0,3:T(8,128)S(1)}, u32[]{:S(2)}) copy-start(f32[8,8,8,8,512]{4,2,1,0,3:T(8,128)S(1)} %copy.111) | copy-start | bytes 25165828
  22.3 28.0 %copy-start.8 = (s32[6,512]{1,0:T(8,128)S(1)}, s32[6,512]{1,0:T(8,128)}, u32[]{:S(2)}) copy-start(s32[6,512]{1,0:T(8,128)} %param.10) | copy-start | bytes 36868
  22.3 28.1 %copy-start.11 = (f32[8]{0:T(128)S(1)}, f32[8]{0:T(128)}, u32[]{:S(2)}) copy-start(f32[8]{0:T(128)} %param.12) | copy-start | bytes 100
  31.2 59.3 %collective-permute-start = (f32[6,8,8,8,512]{4,3,2,1,0:T(8,128)}, f32[6,8,8,8,512]{4,3,2,1,0:T(8,128)}, u32[]{:S(2)}, u32[]{:S(2)}) collective-permute-start(f32[6,8,8,8,512]{4,3,2,1,0:T(8,128)} %bitcast_dynamic-update-slice_fusion.2), channel_id=1, source_target_pairs={{0,1},{1,2},{2,3},{3,4},{4,5},{5,6},{6,7},{7,8},{8,9},{9,10},{10,1... | collective-permute-start | bytes 18874376 | tf_op jit(solution)/shard_map/ppermute | solution.py:18
  36.2 54.3 %collective-permute-start.1 = (f32[6,8,8,8,512]{4,3,2,1,0:T(8,128)}, f32[6,8,8,8,512]{4,3,2,1,0:T(8,128)}, u32[]{:S(2)}, u32[]{:S(2)}) collective-permute-start(f32[6,8,8,8,512]{4,3,2,1,0:T(8,128)} %bitcast_dynamic-update-slice_fusion.2), channel_id=1, source_target_pairs={{1,0},{2,1},{3,2},{4,3},{5,4},{6,5},{7,6},{8,7},{9,8},{10,9},{11,1... | collective-permute-start | bytes 18874376 | tf_op jit(solution)/shard_map/ppermute | solution.py:20
  98.4 13.0 %copy-start.3 = (f32[6,8,8,8,1536]{4,3,2,1,0:T(8,128)}, f32[6,8,8,8,1536]{4,3,2,1,0:T(8,128)S(1)}, u32[]{:S(2)}) copy-start(f32[6,8,8,8,1536]{4,3,2,1,0:T(8,128)S(1)} %pad_maximum_fusion) | copy-start | bytes 56623108
  114.7 15.5 %slice-start.2 = ((s8[8388608]{0:T(1024)(128)(4,1)}), s8[4194304]{0:T(1024)(128)(4,1)S(1)}, s32[]{:S(2)}) async-start(s8[8388608]{0:T(1024)(128)(4,1)} %bitcast.222), calls=%async_computation.3 | async-start | bytes 8388608
  148.6 15.7 %copy-start = (f32[8,8,8,8,512]{4,2,1,0,3:T(8,128)}, f32[8,8,8,8,512]{4,2,1,0,3:T(8,128)S(1)}, u32[]{:S(2)}) copy-start(f32[8,8,8,8,512]{4,2,1,0,3:T(8,128)S(1)} %fusion.6) | copy-start | bytes 25165828
  153.0 101.1 %copy-start.10 = (s32[512]{0:T(512)S(1)}, s32[512]{0:T(512)}, u32[]{:S(2)}) copy-start(s32[512]{0:T(512)} %param.11) | copy-start | bytes 6148
  165.4 128.8 %collective-permute-start.2 = (f32[6,8,8,8,512]{4,3,2,1,0:T(8,128)}, f32[6,8,8,8,512]{4,3,2,1,0:T(8,128)}, u32[]{:S(2)}, u32[]{:S(2)}) collective-permute-start(f32[6,8,8,8,512]{4,3,2,1,0:T(8,128)} %bitcast_dynamic-update-slice_fusion), channel_id=1, source_target_pairs={{0,1},{1,2},{2,3},{3,4},{4,5},{5,6},{6,7},{7,8},{8,9},{9,10},{10,1... | collective-permute-start | bytes 18874376 | tf_op jit(solution)/shard_map/ppermute | solution.py:18
  252.8 41.4 %collective-permute-start.3 = (f32[6,8,8,8,512]{4,3,2,1,0:T(8,128)}, f32[6,8,8,8,512]{4,3,2,1,0:T(8,128)}, u32[]{:S(2)}, u32[]{:S(2)}) collective-permute-start(f32[6,8,8,8,512]{4,3,2,1,0:T(8,128)} %bitcast_dynamic-update-slice_fusion), channel_id=1, source_target_pairs={{1,0},{2,1},{3,2},{4,3},{5,4},{6,5},{7,6},{8,7},{9,8},{10,9},{11,1... | collective-permute-start | bytes 18874376 | tf_op jit(solution)/shard_map/ppermute | solution.py:20
  280.7 27.7 %slice-start = ((s8[8388608]{0:T(1024)(128)(4,1)}), s8[4194304]{0:T(1024)(128)(4,1)S(1)}, s32[]{:S(2)}) async-start(s8[8388608]{0:T(1024)(128)(4,1)} %bitcast.220), calls=%async_computation.1 | async-start | bytes 8388608
  294.1 14.3 %slice-start.1 = ((s8[8388608]{0:T(1024)(128)(4,1)}), s8[4194304]{0:T(1024)(128)(4,1)S(1)}, s32[]{:S(2)}) async-start(s8[8388608]{0:T(1024)(128)(4,1)} %bitcast.220), calls=%async_computation.2 | async-start | bytes 8388608
  324.6 14.6 %copy-start.4 = (f32[8,8,1,8,512]{4,2,1,0,3:T(1,128)S(1)}, f32[8,8,1,8,512]{4,2,1,0,3:T(1,128)}, u32[]{:S(2)}) copy-start(f32[8,8,1,8,512]{4,2,1,0,3:T(1,128)} %get-tuple-element.43) | copy-start | bytes 3145732
  343.5 193.6 %copy-start.7 = (f32[12,256]{1,0:T(8,128)S(1)}, f32[12,256]{1,0:T(8,128)}, u32[]{:S(2)}) copy-start(f32[12,256]{1,0:T(8,128)} %param.13) | copy-start | bytes 36868
  531.9 4.9 collective-permute-start.4
  533.2 3.8 collective-permute-start.5
  568.5 4.4 collective-permute-start.6
  569.8 3.8 collective-permute-start.7
  605.3 4.4 collective-permute-start.8
  606.6 3.8 collective-permute-start.9
  627.4 29.8 %copy-start.9 = (f32[12,256]{1,0:T(8,128)}, f32[12,256]{1,0:T(8,128)S(1)}, u32[]{:S(2)}) copy-start(f32[12,256]{1,0:T(8,128)S(1)} %multiply_add_fusion) | copy-start | bytes 36868
  (3 other events, 18.3 us)
Sparse Core Ops, SparseCore 0:
  368.4 143.9 all-reduce.3
where the time goes:
time: 673 us; the launch traced here: 664 us
  local copies, waits for them, and re-layouts  148 us (22%)
  waiting for transfers between devices  144 us (21%)
  starting transfers between devices  120 us (18%)
  blocking collectives  98.6 us (15%)
  other arithmetic  76 us (11%)
  matrix products  54.6 us (8%)
  between operations  22.8 us (3%)
    unnamed x2, waiting for transfers between devices  142 us
    ppermute x5, starting transfers between devices, with_halo(): lax.ppermute(tail, axis, [(i, (i + 1) % count) for i in range(ends)])  102 us
    dot_general x12, matrix products, ghost_planes(): jnp.dot(flat[face ^ 1], selector, precision=lax.Precision.HIGHEST, prefer...  54.6 us
    unnamed x52, local copies, waits for them, and re-layouts  50.6 us
    psum x3, blocking collectives, squares(): return lax.psum(jnp.sum(residual * residual), 'blk')  40 us
    add x2, other arithmetic, stencil(): u + rates[:, None, None, None, None] * live[None, None, None, None, :] * lap  35.6 us
    psum x2, blocking collectives, on_device(): alpha = norm_now / lax.psum(jnp.sum(direction * image), 'blk')  29.9 us
    slice x2, local copies, waits for them, and re-layouts, stencil(): u[:, :, :, :-1]  27.6 us
  transfers between devices with their start and end apart: 11, of which 4 were waited for; matrix products, arithmetic and copies ran while one was open for 12% of the time, Pallas kernels for 0%

commit v1 on v0

v1 whole, which is shorter than its diff:
```python
import functools

import jax
import jax.numpy as jnp
from jax import lax
from jax.experimental import pallas as pl
from jax.experimental.pallas import tpu as pltpu
from jax.sharding import PartitionSpec as P

ITERS = 3
EDGE = 128
FAR = 1 << 29
PAIR = 2
VMEM_LIMIT = 48 * 1024 * 1024
BF16 = jnp.bfloat16
F32 = jnp.float32


def params():
    return pltpu.CompilerParams(vmem_limit_bytes=VMEM_LIMIT)


def split(x):
    high = x.astype(BF16)
    low = (x - high.astype(F32)).astype(BF16)
    return jnp.concatenate([high, low], axis=0)


def picked(table, selector):
    rows = table.shape[0]
    both = jnp.dot(split(table), selector, preferred_element_type=F32)
    return both[:rows] + both[rows:]


def plane(ref, face):
    end = 0 if face % 2 == 0 else ref.shape[1] - 1
    if face < 2:
        return ref[:, end]
    if face < 4:
        return ref[:, :, end]
    return ref[:, :, :, end, :]


def relative(neighbours, base):
    return jnp.where(neighbours < 0, FAR, neighbours - base)


def one_hot(index, depth):
    rows = lax.broadcasted_iota(jnp.int32, (depth, index.shape[-1]), 0)
    return jnp.where(rows == index, 1.0, 0.0).astype(BF16)


def write_edges(ref, count, head_ref, tail_ref):
    slots = ref.shape[-1]
    lane = lax.broadcasted_iota(jnp.int32, (1, EDGE), 1)
    late = lane + (slots - EDGE) < count
    for face in range(6):
        cells = plane(ref, face)
        head_ref[face] = cells[..., :EDGE]
        tail_ref[face] = jnp.where(
            late, cells[..., slots - EDGE :], cells[..., slots - 2 * EDGE : slots - EDGE]
        )


def edges_kernel(count_ref, u_ref, head_ref, tail_ref):
    write_edges(u_ref, count_ref[0], head_ref, tail_ref)


def step_size(rates_ref, count_ref, var, slots):
    live = lax.broadcasted_iota(jnp.int32, (1, slots), 1) < count_ref[0]
    return jnp.where(live, rates_ref[var], 0.0)


def local_kernel(base_ref, count_ref, rates_ref, near_ref, u_ref, out_ref, selector, ghosts):
    pair, size, _, _, slots = u_ref.shape

    @pl.when(pl.program_id(0) == 0)
    def _():
        for face in range(6):
            index = relative(near_ref[face : face + 1, :], base_ref[0])
            selector[face] = one_hot(index, slots)

    for face in range(6):
        table = plane(u_ref, face ^ 1).reshape(pair * size * size, slots)
        taken = picked(table, selector[face]).reshape(pair, size, size, slots)
        outer = near_ref[face : face + 1, :] < 0
        ghosts[face] = jnp.where(outer, plane(u_ref, face), taken)

    row = lax.broadcasted_iota(jnp.int32, (size, slots), 0)
    first, last = row == 0, row == size - 1

    def variable(v, carry):
        factor = step_size(rates_ref, count_ref, pl.program_id(0) * pair + v, slots)
        for i in range(size):
            for j in range(size):
                cell = u_ref[v, i, j]
                above = u_ref[v, i + 1, j] if i < size - 1 else ghosts[1, v, j]
                below = u_ref[v, i - 1, j] if i > 0 else ghosts[0, v, j]
                right = u_ref[v, i, j + 1] if j < size - 1 else ghosts[3, v, i]
                left = u_ref[v, i, j - 1] if j > 0 else ghosts[2, v, i]
                front = jnp.where(last, ghosts[5, v, i, j : j + 1, :], pltpu.roll(cell, size - 1, 0))
                back = jnp.where(first, ghosts[4, v, i, j : j + 1, :], pltpu.roll(cell, 1, 0))
                lap = ((above + below) + (right + left)) + ((front + back) - 6.0 * cell)
                out_ref[v, i, j] = cell + factor * lap
        return carry

    lax.fori_loop(0, pair, variable, 0)


def remote_body(base_ref, count_ref, rates_ref, near_ref, lower_ref, upper_ref, u_ref, out_ref, selector, ghosts):
    pair, size, _, _, slots = u_ref.shape

    @pl.when(pl.program_id(0) == 0)
    def _():
        for face in range(6):
            index = relative(near_ref[face : face + 1, :], base_ref[0])
            below = jnp.where(index < 0, index & (EDGE - 1), -1)
            beyond = (index >= slots) & (index < FAR)
            index = jnp.where(beyond, index - slots + EDGE, below)
            selector[face] = one_hot(index, 2 * EDGE)

    for face in range(6):
        lower = lower_ref[face ^ 1].reshape(pair * size * size, EDGE)
        upper = upper_ref[face ^ 1].reshape(pair * size * size, EDGE)
        table = jnp.concatenate([lower, upper], axis=1)
        ghosts[face] = picked(table, selector[face]).reshape(pair, size, size, slots)

    row = lax.broadcasted_iota(jnp.int32, (size, slots), 0)
    first, last = row == 0, row == size - 1

    def variable(v, carry):
        factor = step_size(rates_ref, count_ref, pl.program_id(0) * pair + v, slots)
        for i in range(size):
            for j in range(size):
                extra = jnp.where(
                    last,
                    ghosts[5, v, i, j : j + 1, :],
                    jnp.where(first, ghosts[4, v, i, j : j + 1, :], 0.0),
                )
                if i == 0:
                    extra = extra + ghosts[0, v, j]
                if i == size - 1:
                    extra = extra + ghosts[1, v, j]
                if j == 0:
                    extra = extra + ghosts[2, v, i]
                if j == size - 1:
                    extra = extra + ghosts[3, v, i]
                out_ref[v, i, j] = u_ref[v, i, j] + factor * extra
        return carry

    lax.fori_loop(0, pair, variable, 0)


def remote_edges_kernel(base_ref, count_ref, rates_ref, near_ref, lower_ref, upper_ref, u_ref,
                        out_ref, head_ref, tail_ref, selector, ghosts):
    remote_body(base_ref, count_ref, rates_ref, near_ref, lower_ref, upper_ref, u_ref, out_ref, selector, ghosts)
    write_edges(out_ref, count_ref[0], head_ref, tail_ref)


def remote_sums_kernel(base_ref, count_ref, rates_ref, near_ref, lower_ref, upper_ref, u_ref,
                       out_ref, sums_ref, selector, ghosts):
    remote_body(base_ref, count_ref, rates_ref, near_ref, lower_ref, upper_ref, u_ref, out_ref, selector, ghosts)
    for v in range(out_ref.shape[0]):
        sums_ref[0, v : v + 1, :] = jnp.sum(jnp.sum(out_ref[v, 0], axis=0), axis=0, keepdims=True)


def total(x):
    return jnp.sum(x, axis=(0, 1), keepdims=True)


def grid_kernel(shift, first_ref, cells_ref, currents_ref, cond_ref, rows_ref, u_ref, out_ref, share_ref, held):
    lats, lons = cond_ref.shape
    chunks, chunk = cells_ref.shape
    mask = lons - 1

    def gathered(c, acc):
        cell = cells_ref[pl.ds(c, 1), :]
        current = currents_ref[pl.ds(c, 1), :]
        lat = cell >> shift
        lon = cell & mask
        here = lax.broadcasted_iota(jnp.int32, (lats, chunk), 0) == lat
        high = current.astype(BF16).astype(F32)
        low = current - high
        weighted = jnp.concatenate(
            [jnp.where(here, high, 0.0).astype(BF16), jnp.where(here, low, 0.0).astype(BF16)], axis=0
        )
        across = one_hot(lon, lons)
        return acc + lax.dot_general(weighted, across, (((1,), (1,)), ((), ())), preferred_element_type=F32)

    acc = lax.fori_loop(0, chunks, gathered, jnp.zeros((2 * lats, lons), F32))
    source = acc[:lats] + acc[lats:]

    weight = 4.0 + cond_ref[...]
    row = lax.broadcasted_iota(jnp.int32, (lats, lons), 0)
    potential = jnp.zeros_like(source)
    residual = source
    direction = source
    now = total(residual * residual)
    for _ in range(ITERS):
        south = jnp.where(row == 0, 0.0, pltpu.roll(direction, 1, 0))
        north = jnp.where(row == lats - 1, 0.0, pltpu.roll(direction, lats - 1, 0))
        beside = south + north + pltpu.roll(direction, 1, 1) + pltpu.roll(direction, lons - 1, 1)
        image = weight * direction - beside
        alpha = now / total(direction * image)
        potential = potential + alpha * direction
        residual = residual - alpha * image
        new = total(residual * residual)
        direction = residual + (new / now) * direction
        now = new

    held[...] = potential
    for r in range(share_ref.shape[0]):
        share_ref[r : r + 1, :] = held[pl.ds(first_ref[0] + r, 1), :]
    own = rows_ref[...]
    across = picked(potential, one_hot(jnp.where(own < 0, -1, own & mask), lons))
    here = lax.broadcasted_iota(jnp.int32, across.shape, 0) == (own >> shift)
    added = jnp.sum(jnp.where(here, across, 0.0), axis=0, keepdims=True)
    out_ref[...] = u_ref[...] + added


def smem():
    return pl.BlockSpec(memory_space=pltpu.SMEM)


def on_device(state, counts, neighbours, rows, rates, conductance):
    vars_, size, _, _, slots = state.shape
    axes = ("grp", "blk")
    groups, blks = lax.axis_size("grp"), lax.axis_size("blk")
    devices = groups * blks
    blk = lax.axis_index("blk")
    device = lax.axis_index("grp") * blks + blk
    base = jnp.reshape(device * slots, (1,)).astype(jnp.int32)
    grid = (vars_ // PAIR,)
    block = pl.BlockSpec((PAIR, size, size, size, slots), lambda g: (g, 0, 0, 0, 0))
    edge = pl.BlockSpec((6, PAIR, size, size, EDGE), lambda g: (0, g, 0, 0, 0))
    near = pl.BlockSpec(neighbours.shape, lambda g: (0, 0))
    sums = pl.BlockSpec((1, PAIR, slots), lambda g: (g, 0, 0))
    whole = jax.ShapeDtypeStruct(state.shape, F32)
    edge_shape = jax.ShapeDtypeStruct((6, vars_, size, size, EDGE), F32)
    sums_shape = jax.ShapeDtypeStruct((vars_ // PAIR, PAIR, slots), F32)
    ghosts = pltpu.VMEM((6, PAIR, size, size, slots), F32)
    up = [(d, d + 1) for d in range(devices - 1)]
    down = [(d + 1, d) for d in range(devices - 1)]

    def exchange(head, tail):
        return lax.ppermute(tail, axes, up), lax.ppermute(head, axes, down)

    def local(u):
        return pl.pallas_call(
            local_kernel,
            grid=grid,
            in_specs=[smem(), smem(), smem(), near, block],
            out_specs=block,
            out_shape=whole,
            scratch_shapes=[pltpu.VMEM((6, slots, slots), BF16), ghosts],
            compiler_params=params(),
            cost_estimate=pl.CostEstimate(flops=10 * 10**9, bytes_accessed=2 * u.size * 4, transcendentals=0),
            name="local_step",
        )(base, counts, rates, neighbours, u)

    def remote(kernel, u, lower, upper, out_specs, out_shape):
        return pl.pallas_call(
            kernel,
            grid=grid,
            in_specs=[smem(), smem(), smem(), near, edge, edge, block],
            out_specs=[block] + out_specs,
            out_shape=[whole] + out_shape,
            scratch_shapes=[pltpu.VMEM((6, 2 * EDGE, slots), BF16), ghosts],
            compiler_params=params(),
            cost_estimate=pl.CostEstimate(flops=5 * 10**9, bytes_accessed=2 * u.size * 4, transcendentals=0),
            name="remote_step",
        )(base, counts, rates, neighbours, lower, upper, u)

    cells = lax.all_gather(rows, axes, axis=0, tiled=True)
    conduct = lax.all_gather(conductance, "blk", axis=0, tiled=True)

    head, tail = pl.pallas_call(
        edges_kernel,
        grid=grid,
        in_specs=[smem(), block],
        out_specs=[edge, edge],
        out_shape=[edge_shape, edge_shape],
        compiler_params=params(),
        name="edges",
    )(counts, state)
    lower, upper = exchange(head, tail)
    u = local(state)
    u, head, tail = remote(remote_edges_kernel, u, lower, upper, [edge, edge], [edge_shape, edge_shape])
    lower, upper = exchange(head, tail)
    u = local(u)
    u, faces = remote(remote_sums_kernel, u, lower, upper, [sums], [sums_shape])
    faces = faces.reshape(vars_, slots)
    current = (faces[6] - faces[5]) / 8.0
    currents = lax.all_gather(current, axes, axis=0, tiled=True)

    lat_rows, lons = conductance.shape
    chunk = 4 * slots
    first = jnp.reshape(blk * lat_rows, (1,)).astype(jnp.int32)
    face = pl.BlockSpec((1, 1, size, size, slots), lambda g: (1, 0, 0, 0, 0))

    def full(*shape):
        return pl.BlockSpec(shape, lambda g: (0,) * len(shape))

    lats = conduct.shape[0]
    u, share = pl.pallas_call(
        functools.partial(grid_kernel, lons.bit_length() - 1),
        grid=(1,),
        in_specs=[
            smem(),
            full(devices * slots // chunk, chunk),
            full(devices * slots // chunk, chunk),
            full(lats, lons),
            full(1, slots),
            face,
        ],
        out_specs=[face, full(lat_rows, lons)],
        out_shape=[whole, jax.ShapeDtypeStruct(conductance.shape, F32)],
        scratch_shapes=[pltpu.VMEM((lats, lons), F32)],
        input_output_aliases={5: 0},
        compiler_params=params(),
        name="ionosphere",
    )(first, cells.reshape(-1, chunk), currents.reshape(-1, chunk), conduct, rows.reshape(1, slots), u)
    return (u, share)


def solution(mesh):
    placed = (
        P(None, None, None, None, ("grp", "blk")),
        P(("grp", "blk")),
        P(None, ("grp", "blk")),
        P(("grp", "blk")),
        P(),
        P("blk", None),
    )
    return jax.shard_map(
        on_device,
        mesh=mesh,
        in_specs=placed,
        out_specs=(P(None, None, None, None, ("grp", "blk")), P("blk", None)),
        check_vma=False,
    )
```

time: 673 us -> 212 us (0.32); the launches traced: 664 us -> 211 us
  local copies, waits for them, and re-layouts: 148 us -> 0.6 us
  waiting for transfers between devices: 144 us -> 0.01 us
  starting transfers between devices: 120 us -> 27.7 us
  other arithmetic: 76 us -> 0.97 us
  Pallas kernels: 0 us -> 65.4 us
  matrix products: 54.6 us -> 0 us
  between operations: 22.8 us -> 1.42 us
  blocking collectives: 98.6 us -> 115 us
    unnamed x2 -> x0, waiting for transfers between devices: 142 us -> none
    all_gather x1 -> x3, blocking collectives: 9.99 us -> 115 us  [the longest x1 40.3 us: on_device(): cells = lax.all_gather(rows, axes, axis=0, tiled=True)]
    ppermute x10 -> x4, starting transfers between devices: 120 us -> 27.7 us  [exchange(): return (lax.ppermute(tail, axes, up), lax.ppermute(head, axes, down))]
    psum x6 -> x0, blocking collectives: 88.6 us -> none  [the longest x3 40 us: squares(): return lax.psum(jnp.sum(residual * residual), 'blk')]
    slice x20 -> x0, local copies, waits for them, and re-layouts: 86.8 us -> none  [the longest x2 27.6 us: stencil(): u[:, :, :, :-1]]
    pallas_call x0 -> x6, Pallas kernels: none -> 65.4 us  [the longest x2 33.2 us: local(): pl.pallas_call(local_kernel, grid=grid, in_specs=[smem(), smem(), smem(),...]
    dot_general x12 -> x0, matrix products: 54.6 us -> none  [ghost_planes(): jnp.dot(flat[face ^ 1], selector, precision=lax.Precision.HIGHEST, prefer...]
    unnamed x52 -> x9, local copies, waits for them, and re-layouts: 50.6 us -> 0.03 us
  transfers between devices with their start and end apart: 11 -> 4, of which waited for: 4 -> 0; matrix products, arithmetic and copies ran while one was open for 12% -> 0% of each run, Pallas kernels for 0% -> 16%
where the time goes in v1:
time: 212 us; the launch traced here: 211 us
  blocking collectives  115 us (54%)
  Pallas kernels  65.4 us (31%)
  starting transfers between devices  27.7 us (13%)
    all_gather x1, blocking collectives, on_device(): cells = lax.all_gather(rows, axes, axis=0, tiled=True)  40.3 us
    all_gather x1, blocking collectives, on_device(): conduct = lax.all_gather(conductance, 'blk', axis=0, tiled=True)  38 us
    all_gather x1, blocking collectives, on_device(): currents = lax.all_gather(current, axes, axis=0, tiled=True)  36.8 us
    pallas_call x2, Pallas kernels, local(): pl.pallas_call(local_kernel, grid=grid, in_specs=[smem(), smem(), smem(),...  33.2 us
    ppermute x4, starting transfers between devices, exchange(): return (lax.ppermute(tail, axes, up), lax.ppermute(head, axes, down))  27.7 us
    pallas_call x2, Pallas kernels, remote(): pl.pallas_call(kernel, grid=grid, in_specs=[smem(), smem(), smem(), near,...  19.7 us
    pallas_call x1, Pallas kernels, on_device(): pl.pallas_call(functools.partial(grid_kernel, lons.bit_length() - 1), gri...  7.18 us
    pallas_call x1, Pallas kernels, on_device(): pl.pallas_call(edges_kernel, grid=grid, in_specs=[smem(), block], out_spe...  5.39 us
  transfers between devices with their start and end apart: 4, of which 0 were waited for; matrix products, arithmetic and copies ran while one was open for 0% of the time, Pallas kernels for 16%

profile of v1, /device:TPU:0, one launch (start us, length us, event | category | flops | bytes accessed | tf_op | source)
XLA Modules:
  0.0 211.2 jit_solution(10465666219077422472)
XLA Ops:
  1.3 0.0 copy-start.1
  1.3 0.0 copy-start.2
  1.3 5.4 %edges.1 = (f32[6,8,8,8,128]{4,3,2,1,0:T(8,128)S(1)}, f32[6,8,8,8,128]{4,3,2,1,0:T(8,128)}) custom-call(s32[1]{0:T(128)S(6)} %copy.10.count_ref, f32[8,8,8,8,512]{4,3,2,1,0:T(8,128)} %u_ref.3), custom_call_target="tpu_custom_call" | custom-call | tf_op jit(solution)/shard_map/edges/pallas_call | solution.py:277
  6.7 2.4 %collective-permute-start = (f32[6,8,8,8,128]{4,3,2,1,0:T(8,128)}, f32[6,8,8,8,128]{4,3,2,1,0:T(8,128)S(1)}, u32[]{:S(2)}, u32[]{:S(2)}) collective-permute-start(f32[6,8,8,8,128]{4,3,2,1,0:T(8,128)} %get-tuple-element.9), channel_id=1, source_target_pairs={{0,1},{1,2},{2,3},{3,4},{4,5},{5,6},{6,7},{7,8},{8,9},{9,10},{10,1... | collective-permute-start | bytes 4718600 | tf_op jit(solution)/shard_map/ppermute | solution.py:246
  9.1 1.3 collective-permute-start.1
  10.4 0.0 copy-done.1
  10.5 16.6 %local_step.2.u_ref = f32[8,8,8,8,512]{4,3,2,1,0:T(8,128)} custom-call(s32[1]{0:T(128)} %bitcast.2.base_ref, s32[1]{0:T(128)S(6)} %copy.10.count_ref, f32[8]{0:T(128)S(1)} %copy-done.2, s32[6,512]{1,0:T(8,128)S(1)} %copy-done.1, f32[8,8,8,8,512]{4,3,2,1,0:T(8,128)} %u_ref.3), custom_call_target="tpu_custom_call" | custom-call | flops 10000000000 | bytes 16777216 | tf_op jit(solution)/shard_map/local_step/pallas_call | solution.py:249
  27.1 0.0 collective-permute-done.lower_ref
  27.1 0.0 collective-permute-done.1.upper_ref
  27.1 10.1 %remote_step.2 = (f32[8,8,8,8,512]{4,3,2,1,0:T(8,128)}, f32[6,8,8,8,128]{4,3,2,1,0:T(8,128)S(1)}, f32[6,8,8,8,128]{4,3,2,1,0:T(8,128)}) custom-call(s32[1]{0:T(128)} %bitcast.2.base_ref, s32[1]{0:T(128)S(6)} %copy.10.count_ref, f32[8]{0:T(128)S(1)} %copy-done.2, s32[6,512]{1,0:T(8,128)S(1)} %copy-done.1, ...), custom_call_target="tpu_custom_call" | custom-call | flops 5000000000 | bytes 16777216 | tf_op jit(solution)/shard_map/remote_step/pallas_call | solution.py:262
  37.2 22.7 %collective-permute-start.2 = (f32[6,8,8,8,128]{4,3,2,1,0:T(8,128)}, f32[6,8,8,8,128]{4,3,2,1,0:T(8,128)S(1)}, u32[]{:S(2)}, u32[]{:S(2)}) collective-permute-start(f32[6,8,8,8,128]{4,3,2,1,0:T(8,128)} %get-tuple-element.11), channel_id=1, source_target_pairs={{0,1},{1,2},{2,3},{3,4},{4,5},{5,6},{6,7},{7,8},{8,9},{9,10},{10,1... | collective-permute-start | bytes 4718600 | tf_op jit(solution)/shard_map/ppermute | solution.py:246
  59.9 1.3 collective-permute-start.3
  61.2 0.0 copy-done.3
  61.2 38.0 %all-gather.2 = f32[8,12,256]{2,1,0:T(8,128)S(1)} all-gather(f32[1,12,256]{2,1,0:T(8,128)S(1)} %bitcast.7), channel_id=1, replica_groups=mesh['grp'=4,'blk'=8] {'blk'}, dimensions={0}, use_global_device_ids=true | all-gather | bytes 110592 | tf_op jit(solution)/shard_map/all_gather | solution.py:275
  99.3 40.3 %all-gather.1 = s32[32,1,512]{2,1,0:T(1,128)S(1)} all-gather(s32[1,1,512]{2,1,0:T(1,128)S(1)} %bitcast.5), channel_id=1, replica_groups=mesh['grp'=4,'blk'=8] {'grp','blk'}, dimensions={0}, use_global_device_ids=true | all-gather | bytes 67584 | tf_op jit(solution)/shard_map/all_gather | solution.py:274
  139.5 0.2 reduce
  139.7 16.6 %local_step.3.u_ref = f32[8,8,8,8,512]{4,3,2,1,0:T(8,128)} custom-call(s32[1]{0:T(128)} %bitcast.2.base_ref, s32[1]{0:T(128)S(6)} %copy.10.count_ref, f32[8]{0:T(128)S(1)} %copy-done.2, s32[6,512]{1,0:T(8,128)S(1)} %copy-done.1, f32[8,8,8,8,512]{4,3,2,1,0:T(8,128)} %get-tuple-element.13.u_ref), custom_call_target="tpu_custom_call" | custom-call | flops 10000000000 | bytes 16777216 | tf_op jit(solution)/shard_map/local_step/pallas_call | solution.py:249
  156.3 0.0 collective-permute-done.2.lower_ref
  156.3 0.0 collective-permute-done.3.upper_ref
  156.3 9.5 %remote_step.3 = (f32[8,8,8,8,512]{4,3,2,1,0:T(8,128)}, f32[4,2,512]{2,1,0:T(2,128)S(1)}) custom-call(s32[1]{0:T(128)} %bitcast.2.base_ref, s32[1]{0:T(128)S(6)} %copy.10.count_ref, f32[8]{0:T(128)S(1)} %copy-done.2, s32[6,512]{1,0:T(8,128)S(1)} %copy-done.1, f32[6,8,8,8,128]{4,3,2,1,0:T(8,128)S(1)} %collective-permute-done.2.lower_ref, ...), custom_call_target="tpu_custom_call" | custom-call | flops 5000000000 | bytes 16777216 | tf_op jit(solution)/shard_map/remote_step/pallas_call | solution.py:262
  165.9 36.8 %all-gather = f32[1,16384]{1,0:T(1,128)S(1)} all-gather(f32[1,512]{1,0:T(1,128)S(1)} %fusion), channel_id=2, replica_groups=mesh['grp'=4,'blk'=8] {'grp','blk'}, dimensions={1}, use_global_device_ids=true | all-gather | bytes 67584 | tf_op jit(solution)/shard_map/all_gather | solution.py:294
  202.7 0.5 broadcast.7
  203.2 0.8 reduce.4
  204.0 7.2 %ionosphere.1 = (f32[8,8,8,8,512]{4,3,2,1,0:T(8,128)}, f32[12,256]{1,0:T(8,128)}) custom-call(s32[1]{0:T(128)} %bitcast.first_ref, s32[8,2048]{1,0:T(8,128)S(1)} %reshape.26.cells_ref, f32[8,2048]{1,0:T(8,128)S(1)} %reshape.29.currents_ref, f32[96,256]{1,0:T(8,128)S(1)} %reshape.36.cond_ref, s32[1,512]{1,0:T(1,128)S(1)} %bitcast.6, ...), custom_call_target="tpu_custom_call", output_to_operand_aliasing={{0}: (5, {})} | custom-call | tf_op jit(solution)/shard_map/ionosphere/pallas_call | solution.py:305
  (9 shorter events, 0.1 us)
Async XLA Ops:
  1.3 9.2 %copy-start.1 = (s32[6,512]{1,0:T(8,128)S(1)}, s32[6,512]{1,0:T(8,128)}, u32[]{:S(2)}) copy-start(s32[6,512]{1,0:T(8,128)} %near_ref.7) | copy-start | bytes 36868
  1.3 9.2 %copy-start.2 = (f32[8]{0:T(128)S(1)}, f32[8]{0:T(128)}, u32[]{:S(2)}) copy-start(f32[8]{0:T(128)} %rates_ref.7) | copy-start | bytes 100
  6.7 20.4 %collective-permute-start = (f32[6,8,8,8,128]{4,3,2,1,0:T(8,128)}, f32[6,8,8,8,128]{4,3,2,1,0:T(8,128)S(1)}, u32[]{:S(2)}, u32[]{:S(2)}) collective-permute-start(f32[6,8,8,8,128]{4,3,2,1,0:T(8,128)} %get-tuple-element.9), channel_id=1, source_target_pairs={{0,1},{1,2},{2,3},{3,4},{4,5},{5,6},{6,7},{7,8},{8,9},{9,10},{10,1... | collective-permute-start | bytes 4718600 | tf_op jit(solution)/shard_map/ppermute | solution.py:246
  9.1 17.9 %collective-permute-start.1 = (f32[6,8,8,8,128]{4,3,2,1,0:T(8,128)S(1)}, f32[6,8,8,8,128]{4,3,2,1,0:T(8,128)}, u32[]{:S(2)}, u32[]{:S(2)}) collective-permute-start(f32[6,8,8,8,128]{4,3,2,1,0:T(8,128)S(1)} %get-tuple-element.10), channel_id=1, source_target_pairs={{1,0},{2,1},{3,2},{4,3},{5,4},{6,5},{7,6},{8,7},{9,8},{10,9},{11,1... | collective-permute-start | bytes 4718600 | tf_op jit(solution)/shard_map/ppermute | solution.py:246
  27.1 34.2 %copy-start.3 = (f32[12,256]{1,0:T(8,128)S(1)}, f32[12,256]{1,0:T(8,128)}, u32[]{:S(2)}) copy-start(f32[12,256]{1,0:T(8,128)} %param.11) | copy-start | bytes 36868
  27.1 72.2 %copy-start = (s32[512]{0:T(512)S(1)}, s32[512]{0:T(512)}, u32[]{:S(2)}) copy-start(s32[512]{0:T(512)} %param.9) | copy-start | bytes 6148
  37.2 119.1 %collective-permute-start.2 = (f32[6,8,8,8,128]{4,3,2,1,0:T(8,128)}, f32[6,8,8,8,128]{4,3,2,1,0:T(8,128)S(1)}, u32[]{:S(2)}, u32[]{:S(2)}) collective-permute-start(f32[6,8,8,8,128]{4,3,2,1,0:T(8,128)} %get-tuple-element.11), channel_id=1, source_target_pairs={{0,1},{1,2},{2,3},{3,4},{4,5},{5,6},{6,7},{7,8},{8,9},{9,10},{10,1... | collective-permute-start | bytes 4718600 | tf_op jit(solution)/shard_map/ppermute | solution.py:246
  59.9 96.4 %collective-permute-start.3 = (f32[6,8,8,8,128]{4,3,2,1,0:T(8,128)S(1)}, f32[6,8,8,8,128]{4,3,2,1,0:T(8,128)}, u32[]{:S(2)}, u32[]{:S(2)}) collective-permute-start(f32[6,8,8,8,128]{4,3,2,1,0:T(8,128)S(1)} %get-tuple-element.12), channel_id=1, source_target_pairs={{1,0},{2,1},{3,2},{4,3},{5,4},{6,5},{7,6},{8,7},{9,8},{10,9},{11,1... | collective-permute-start | bytes 4718600 | tf_op jit(solution)/shard_map/ppermute | solution.py:246

commit v2 on v1

--- a/solution.py
+++ b/solution.py
@@ -168,26 +168,90 @@
     return jnp.sum(x, axis=(0, 1), keepdims=True)
 
 
-def grid_kernel(shift, first_ref, cells_ref, currents_ref, cond_ref, rows_ref, u_ref, out_ref, share_ref, held):
+def spread_kernel(groups, blks, rows_ref, faces_ref, cond_ref, parts_ref, whole_ref,
+                  packet, landed, slabs, send_sem, recv_sem, slab_send_sem, slab_recv_sem):
+    devices = groups * blks
+    grp, blk = lax.axis_index("grp"), lax.axis_index("blk")
+    me = grp * blks + blk
+
+    def place(step):
+        other = lax.rem(me + step, devices)
+        return (other // blks, lax.rem(other, blks))
+
+    def along(step):
+        return (grp, lax.rem(blk + step, blks))
+
+    barrier = pltpu.get_barrier_semaphore()
+
+    def greet(step, carry):
+        pl.semaphore_signal(barrier, inc=1, device_id=place(step), device_id_type=pl.DeviceIdType.MESH)
+        return carry
+
+    lax.fori_loop(1, devices, greet, 0)
+    packet[0:1, :] = rows_ref[...].astype(F32)
+    packet[1:2, :] = (faces_ref[6:7, :] - faces_ref[5:6, :]) / 8.0
+    pl.semaphore_wait(barrier, devices - 1)
+
+    def copy(step):
+        return pltpu.make_async_remote_copy(
+            src_ref=packet, dst_ref=landed.at[me], send_sem=send_sem.at[step], recv_sem=recv_sem.at[step],
+            device_id=place(step), device_id_type=pl.DeviceIdType.MESH)
+
+    def slab_copy(step):
+        return pltpu.make_async_remote_copy(
+            src_ref=cond_ref, dst_ref=slabs.at[blk], send_sem=slab_send_sem.at[step],
+            recv_sem=slab_recv_sem.at[step], device_id=along(step), device_id_type=pl.DeviceIdType.MESH)
+
+    def start(step, carry):
+        copy(step).start()
+        return carry
+
+    def start_slab(step, carry):
+        slab_copy(step).start()
+        return carry
+
+    def finish(step, carry):
+        copy(step).wait()
+        return carry
+
+    def finish_slab(step, carry):
+        slab_copy(step).wait()
+        return carry
+
+    lax.fori_loop(1, devices, start, 0)
+    lax.fori_loop(1, blks, start_slab, 0)
+    landed[me] = packet[...]
+    slabs[blk] = cond_ref[...]
+    lax.fori_loop(1, devices, finish, 0)
+    lax.fori_loop(1, blks, finish_slab, 0)
+    parts_ref[...] = landed[...]
+    lats = cond_ref.shape[0]
+    for b in range(blks):
+        whole_ref[b * lats : (b + 1) * lats, :] = slabs[b]
+
+
+def grid_kernel(shift, first_ref, parts_ref, cond_ref, rows_ref, u_ref, out_ref, share_ref, held):
     lats, lons = cond_ref.shape
-    chunks, chunk = cells_ref.shape
+    devices, _, slots = parts_ref.shape
     mask = lons - 1
 
     def gathered(c, acc):
-        cell = cells_ref[pl.ds(c, 1), :]
-        current = currents_ref[pl.ds(c, 1), :]
-        lat = cell >> shift
-        lon = cell & mask
-        here = lax.broadcasted_iota(jnp.int32, (lats, chunk), 0) == lat
-        high = current.astype(BF16).astype(F32)
-        low = current - high
-        weighted = jnp.concatenate(
-            [jnp.where(here, high, 0.0).astype(BF16), jnp.where(here, low, 0.0).astype(BF16)], axis=0
-        )
-        across = one_hot(lon, lons)
-        return acc + lax.dot_general(weighted, across, (((1,), (1,)), ((), ())), preferred_element_type=F32)
-
-    acc = lax.fori_loop(0, chunks, gathered, jnp.zeros((2 * lats, lons), F32))
+        for part in range(4):
+            piece = parts_ref[c * 4 + part]
+            cell = piece[0:1, :].astype(jnp.int32)
+            current = piece[1:2, :]
+            here = lax.broadcasted_iota(jnp.int32, (lats, slots), 0) == (cell >> shift)
+            high = current.astype(BF16).astype(F32)
+            low = current - high
+            weighted = jnp.concatenate(
+                [jnp.where(here, high, 0.0).astype(BF16), jnp.where(here, low, 0.0).astype(BF16)], axis=0
+            )
+            across = one_hot(cell & mask, lons)
+            acc = acc + lax.dot_general(
+                weighted, across, (((1,), (1,)), ((), ())), preferred_element_type=F32)
+        return acc
+
+    acc = lax.fori_loop(0, devices // 4, gathered, jnp.zeros((2 * lats, lons), F32))
     source = acc[:lats] + acc[lats:]
 
     weight = 4.0 + cond_ref[...]
@@ -271,9 +335,6 @@
             name="remote_step",
         )(base, counts, rates, neighbours, lower, upper, u)
 
-    cells = lax.all_gather(rows, axes, axis=0, tiled=True)
-    conduct = lax.all_gather(conductance, "blk", axis=0, tiled=True)
-
     head, tail = pl.pallas_call(
         edges_kernel,
         grid=grid,
@@ -289,26 +350,40 @@
     lower, upper = exchange(head, tail)
     u = local(u)
     u, faces = remote(remote_sums_kernel, u, lower, upper, [sums], [sums_shape])
-    faces = faces.reshape(vars_, slots)
-    current = (faces[6] - faces[5]) / 8.0
-    currents = lax.all_gather(current, axes, axis=0, tiled=True)
-
     lat_rows, lons = conductance.shape
-    chunk = 4 * slots
+    lats = lat_rows * blks
+    own_rows = rows.reshape(1, slots)
+    parts, conduct = pl.pallas_call(
+        functools.partial(spread_kernel, groups, blks),
+        in_specs=[pl.BlockSpec(memory_space=pltpu.VMEM)] * 3,
+        out_specs=[pl.BlockSpec(memory_space=pltpu.VMEM)] * 2,
+        out_shape=[jax.ShapeDtypeStruct((devices, 2, slots), F32), jax.ShapeDtypeStruct((lats, lons), F32)],
+        scratch_shapes=[
+            pltpu.VMEM((2, slots), F32),
+            pltpu.VMEM((devices, 2, slots), F32),
+            pltpu.VMEM((blks, lat_rows, lons), F32),
+            pltpu.SemaphoreType.DMA((devices,)),
+            pltpu.SemaphoreType.DMA((devices,)),
+            pltpu.SemaphoreType.DMA((blks,)),
+            pltpu.SemaphoreType.DMA((blks,)),
+        ],
+        compiler_params=pltpu.CompilerParams(
+            vmem_limit_bytes=VMEM_LIMIT, collective_id=0, has_side_effects=True),
+        name="spread",
+    )(own_rows, faces.reshape(vars_, slots), conductance)
+
     first = jnp.reshape(blk * lat_rows, (1,)).astype(jnp.int32)
     face = pl.BlockSpec((1, 1, size, size, slots), lambda g: (1, 0, 0, 0, 0))
 
     def full(*shape):
         return pl.BlockSpec(shape, lambda g: (0,) * len(shape))
 
-    lats = conduct.shape[0]
     u, share = pl.pallas_call(
         functools.partial(grid_kernel, lons.bit_length() - 1),
         grid=(1,),
         in_specs=[
             smem(),
-            full(devices * slots // chunk, chunk),
-            full(devices * slots // chunk, chunk),
+            full(devices, 2, slots),
             full(lats, lons),
             full(1, slots),
             face,
@@ -316,10 +391,10 @@
         out_specs=[face, full(lat_rows, lons)],
         out_shape=[whole, jax.ShapeDtypeStruct(conductance.shape, F32)],
         scratch_shapes=[pltpu.VMEM((lats, lons), F32)],
-        input_output_aliases={5: 0},
+        input_output_aliases={4: 0},
         compiler_params=params(),
         name="ionosphere",
-    )(first, cells.reshape(-1, chunk), currents.reshape(-1, chunk), conduct, rows.reshape(1, slots), u)
+    )(first, parts, conduct, own_rows, u)
     return (u, share)
 
 

time: 212 us -> 123 us (0.58)
  blocking collectives: 115 us -> 0 us
  Pallas kernels: 65.4 us -> 93.6 us
    all_gather x3 -> x0, blocking collectives: 115 us -> none  [the longest x1 40.3 us: on_device(): cells = lax.all_gather(rows, axes, axis=0, tiled=True)]
    pallas_call x0 -> x1, Pallas kernels: none -> 28.3 us  [on_device(): pl.pallas_call(functools.partial(spread_kernel, groups, blks), in_specs=[...]
  transfers between devices with their start and end apart: 4 -> 4, of which waited for: 0 -> 0; matrix products, arithmetic and copies ran while one was open for 0% -> 0% of each run, Pallas kernels for 16% -> 27%
where the time goes in v2:
time: 123 us
  Pallas kernels  93.6 us (76%)
  starting transfers between devices  27.7 us (23%)
  between operations  1.39 us (1%)
    pallas_call x2, Pallas kernels, local(): pl.pallas_call(local_kernel, grid=grid, in_specs=[smem(), smem(), smem(),...  33.1 us
    pallas_call x1, Pallas kernels, on_device(): pl.pallas_call(functools.partial(spread_kernel, groups, blks), in_specs=[...  28.3 us
    ppermute x4, starting transfers between devices, exchange(): return (lax.ppermute(tail, axes, up), lax.ppermute(head, axes, down))  27.7 us
    pallas_call x2, Pallas kernels, remote(): pl.pallas_call(kernel, grid=grid, in_specs=[smem(), smem(), smem(), near,...  19.6 us
    pallas_call x1, Pallas kernels, on_device(): pl.pallas_call(functools.partial(grid_kernel, lons.bit_length() - 1), gri...  7.18 us
    pallas_call x1, Pallas kernels, on_device(): pl.pallas_call(edges_kernel, grid=grid, in_specs=[smem(), block], out_spe...  5.41 us
  transfers between devices with their start and end apart: 4, of which 0 were waited for; matrix products, arithmetic and copies ran while one was open for 0% of the time, Pallas kernels for 27%

profile of v2, /device:TPU:0, one launch (start us, length us, event | category | flops | bytes accessed | tf_op | source)
XLA Modules:
  0.0 122.8 jit_solution(6911878101203945879)
XLA Ops:
  1.3 0.0 copy-start.2
  1.3 0.0 copy-start.3
  1.3 5.4 %edges.1 = (f32[6,8,8,8,128]{4,3,2,1,0:T(8,128)S(1)}, f32[6,8,8,8,128]{4,3,2,1,0:T(8,128)}) custom-call(s32[1]{0:T(128)S(6)} %copy.10.count_ref, f32[8,8,8,8,512]{4,3,2,1,0:T(8,128)} %u_ref.3), custom_call_target="tpu_custom_call" | custom-call | tf_op jit(solution)/shard_map/edges/pallas_call | solution.py:338
  6.7 2.4 %collective-permute-start = (f32[6,8,8,8,128]{4,3,2,1,0:T(8,128)}, f32[6,8,8,8,128]{4,3,2,1,0:T(8,128)S(1)}, u32[]{:S(2)}, u32[]{:S(2)}) collective-permute-start(f32[6,8,8,8,128]{4,3,2,1,0:T(8,128)} %get-tuple-element.11), channel_id=1, source_target_pairs={{0,1},{1,2},{2,3},{3,4},{4,5},{5,6},{6,7},{7,8},{8,9},{9,10},{10,1... | collective-permute-start | bytes 4718600 | tf_op jit(solution)/shard_map/ppermute | solution.py:310
  9.2 1.3 %collective-permute-start.1 = (f32[6,8,8,8,128]{4,3,2,1,0:T(8,128)S(1)}, f32[6,8,8,8,128]{4,3,2,1,0:T(8,128)}, u32[]{:S(2)}, u32[]{:S(2)}) collective-permute-start(f32[6,8,8,8,128]{4,3,2,1,0:T(8,128)S(1)} %get-tuple-element.12), channel_id=1, source_target_pairs={{1,0},{2,1},{3,2},{4,3},{5,4},{6,5},{7,6},{8,7},{9,8},{10,9},{11,1... | collective-permute-start | bytes 4718600 | tf_op jit(solution)/shard_map/ppermute | solution.py:310
  10.5 0.0 copy-done.2
  10.5 0.0 copy-done.3
  10.5 16.6 %local_step.2.u_ref = f32[8,8,8,8,512]{4,3,2,1,0:T(8,128)} custom-call(s32[1]{0:T(128)} %bitcast.2.base_ref, s32[1]{0:T(128)S(6)} %copy.10.count_ref, f32[8]{0:T(128)S(1)} %copy-done.3, s32[6,512]{1,0:T(8,128)S(1)} %copy-done.2, f32[8,8,8,8,512]{4,3,2,1,0:T(8,128)} %u_ref.3), custom_call_target="tpu_custom_call" | custom-call | flops 10000000000 | bytes 16777216 | tf_op jit(solution)/shard_map/local_step/pallas_call | solution.py:313
  27.1 0.0 collective-permute-done.lower_ref
  27.1 0.0 collective-permute-done.1.upper_ref
  27.1 10.1 %remote_step.2 = (f32[8,8,8,8,512]{4,3,2,1,0:T(8,128)}, f32[6,8,8,8,128]{4,3,2,1,0:T(8,128)S(1)}, f32[6,8,8,8,128]{4,3,2,1,0:T(8,128)}) custom-call(s32[1]{0:T(128)} %bitcast.2.base_ref, s32[1]{0:T(128)S(6)} %copy.10.count_ref, f32[8]{0:T(128)S(1)} %copy-done.3, s32[6,512]{1,0:T(8,128)S(1)} %copy-done.2, ...), custom_call_target="tpu_custom_call" | custom-call | flops 5000000000 | bytes 16777216 | tf_op jit(solution)/shard_map/remote_step/pallas_call | solution.py:326
  37.2 22.7 %collective-permute-start.2 = (f32[6,8,8,8,128]{4,3,2,1,0:T(8,128)}, f32[6,8,8,8,128]{4,3,2,1,0:T(8,128)S(1)}, u32[]{:S(2)}, u32[]{:S(2)}) collective-permute-start(f32[6,8,8,8,128]{4,3,2,1,0:T(8,128)} %get-tuple-element.13), channel_id=1, source_target_pairs={{0,1},{1,2},{2,3},{3,4},{4,5},{5,6},{6,7},{7,8},{8,9},{9,10},{10,1... | collective-permute-start | bytes 4718600 | tf_op jit(solution)/shard_map/ppermute | solution.py:310
  59.9 1.3 %collective-permute-start.3 = (f32[6,8,8,8,128]{4,3,2,1,0:T(8,128)S(1)}, f32[6,8,8,8,128]{4,3,2,1,0:T(8,128)}, u32[]{:S(2)}, u32[]{:S(2)}) collective-permute-start(f32[6,8,8,8,128]{4,3,2,1,0:T(8,128)S(1)} %get-tuple-element.14), channel_id=1, source_target_pairs={{1,0},{2,1},{3,2},{4,3},{5,4},{6,5},{7,6},{8,7},{9,8},{10,9},{11,1... | collective-permute-start | bytes 4718600 | tf_op jit(solution)/shard_map/ppermute | solution.py:310
  61.2 16.6 %local_step.3.u_ref = f32[8,8,8,8,512]{4,3,2,1,0:T(8,128)} custom-call(s32[1]{0:T(128)} %bitcast.2.base_ref, s32[1]{0:T(128)S(6)} %copy.10.count_ref, f32[8]{0:T(128)S(1)} %copy-done.3, s32[6,512]{1,0:T(8,128)S(1)} %copy-done.2, f32[8,8,8,8,512]{4,3,2,1,0:T(8,128)} %get-tuple-element.15.u_ref), custom_call_target="tpu_custom_call" | custom-call | flops 10000000000 | bytes 16777216 | tf_op jit(solution)/shard_map/local_step/pallas_call | solution.py:313
  77.8 0.0 copy-start
  77.8 0.0 copy-start.1
  77.8 0.0 collective-permute-done.2.lower_ref
  77.8 0.0 collective-permute-done.3.upper_ref
  77.8 9.5 %remote_step.3 = (f32[8,8,8,8,512]{4,3,2,1,0:T(8,128)}, f32[4,2,512]{2,1,0:T(2,128)S(1)}) custom-call(s32[1]{0:T(128)} %bitcast.2.base_ref, s32[1]{0:T(128)S(6)} %copy.10.count_ref, f32[8]{0:T(128)S(1)} %copy-done.3, s32[6,512]{1,0:T(8,128)S(1)} %copy-done.2, f32[6,8,8,8,128]{4,3,2,1,0:T(8,128)S(1)} %collective-permute-done.2.lower_ref, ...), custom_call_target="tpu_custom_call" | custom-call | flops 5000000000 | bytes 16777216 | tf_op jit(solution)/shard_map/remote_step/pallas_call | solution.py:326
  87.3 0.0 copy-done
  87.3 0.0 copy-done.1
  87.3 28.3 %spread.1 = (f32[32,2,512]{2,1,0:T(2,128)S(1)}, f32[96,256]{1,0:T(8,128)S(1)}) custom-call(s32[1,512]{1,0:T(1,128)S(1)} %bitcast.3, f32[8,512]{1,0:T(8,128)S(1)} %reshape.19.faces_ref, f32[12,256]{1,0:T(8,128)S(1)} %copy-done), custom_call_target="tpu_custom_call" | custom-call | tf_op jit(solution)/shard_map/spread/pallas_call | solution.py:356
  115.6 7.2 %ionosphere.1 = (f32[8,8,8,8,512]{4,3,2,1,0:T(8,128)}, f32[12,256]{1,0:T(8,128)}) custom-call(s32[1]{0:T(128)} %bitcast.first_ref, f32[32,2,512]{2,1,0:T(2,128)S(1)} %get-tuple-element.17.parts_ref, f32[96,256]{1,0:T(8,128)S(1)} %get-tuple-element.18.cond_ref, s32[1,512]{1,0:T(1,128)S(1)} %bitcast.4, ...), custom_call_target="tpu_custom_call", output_to_operand_aliasing={{0}: (4, {})} | custom-call | tf_op jit(solution)/shard_map/ionosphere/pallas_call | solution.py:381
  (1 shorter events, 0.0 us)
Async XLA Ops:
  1.3 9.2 %copy-start.2 = (s32[6,512]{1,0:T(8,128)S(1)}, s32[6,512]{1,0:T(8,128)}, u32[]{:S(2)}) copy-start(s32[6,512]{1,0:T(8,128)} %near_ref.7) | copy-start | bytes 36868
  1.3 9.2 %copy-start.3 = (f32[8]{0:T(128)S(1)}, f32[8]{0:T(128)}, u32[]{:S(2)}) copy-start(f32[8]{0:T(128)} %rates_ref.7) | copy-start | bytes 100
  6.7 20.4 %collective-permute-start = (f32[6,8,8,8,128]{4,3,2,1,0:T(8,128)}, f32[6,8,8,8,128]{4,3,2,1,0:T(8,128)S(1)}, u32[]{:S(2)}, u32[]{:S(2)}) collective-permute-start(f32[6,8,8,8,128]{4,3,2,1,0:T(8,128)} %get-tuple-element.11), channel_id=1, source_target_pairs={{0,1},{1,2},{2,3},{3,4},{4,5},{5,6},{6,7},{7,8},{8,9},{9,10},{10,1... | collective-permute-start | bytes 4718600 | tf_op jit(solution)/shard_map/ppermute | solution.py:310
  9.2 17.9 %collective-permute-start.1 = (f32[6,8,8,8,128]{4,3,2,1,0:T(8,128)S(1)}, f32[6,8,8,8,128]{4,3,2,1,0:T(8,128)}, u32[]{:S(2)}, u32[]{:S(2)}) collective-permute-start(f32[6,8,8,8,128]{4,3,2,1,0:T(8,128)S(1)} %get-tuple-element.12), channel_id=1, source_target_pairs={{1,0},{2,1},{3,2},{4,3},{5,4},{6,5},{7,6},{8,7},{9,8},{10,9},{11,1... | collective-permute-start | bytes 4718600 | tf_op jit(solution)/shard_map/ppermute | solution.py:310
  37.2 40.6 %collective-permute-start.2 = (f32[6,8,8,8,128]{4,3,2,1,0:T(8,128)}, f32[6,8,8,8,128]{4,3,2,1,0:T(8,128)S(1)}, u32[]{:S(2)}, u32[]{:S(2)}) collective-permute-start(f32[6,8,8,8,128]{4,3,2,1,0:T(8,128)} %get-tuple-element.13), channel_id=1, source_target_pairs={{0,1},{1,2},{2,3},{3,4},{4,5},{5,6},{6,7},{7,8},{8,9},{9,10},{10,1... | collective-permute-start | bytes 4718600 | tf_op jit(solution)/shard_map/ppermute | solution.py:310
  59.9 17.9 %collective-permute-start.3 = (f32[6,8,8,8,128]{4,3,2,1,0:T(8,128)S(1)}, f32[6,8,8,8,128]{4,3,2,1,0:T(8,128)}, u32[]{:S(2)}, u32[]{:S(2)}) collective-permute-start(f32[6,8,8,8,128]{4,3,2,1,0:T(8,128)S(1)} %get-tuple-element.14), channel_id=1, source_target_pairs={{1,0},{2,1},{3,2},{4,3},{5,4},{6,5},{7,6},{8,7},{9,8},{10,9},{11,1... | collective-permute-start | bytes 4718600 | tf_op jit(solution)/shard_map/ppermute | solution.py:310
  77.8 9.6 %copy-start = (f32[12,256]{1,0:T(8,128)S(1)}, f32[12,256]{1,0:T(8,128)}, u32[]{:S(2)}) copy-start(f32[12,256]{1,0:T(8,128)} %cond_ref.1) | copy-start | bytes 36868
  77.8 9.6 %copy-start.1 = (s32[512]{0:T(512)S(1)}, s32[512]{0:T(512)}, u32[]{:S(2)}) copy-start(s32[512]{0:T(512)} %param.9) | copy-start | bytes 6148

commit v3 on v2

--- a/solution.py
+++ b/solution.py
@@ -41,47 +41,73 @@
     return ref[:, :, :, end, :]
 
 
-def relative(neighbours, base):
-    return jnp.where(neighbours < 0, FAR, neighbours - base)
-
-
 def one_hot(index, depth):
     rows = lax.broadcasted_iota(jnp.int32, (depth, index.shape[-1]), 0)
     return jnp.where(rows == index, 1.0, 0.0).astype(BF16)
 
 
 def write_edges(ref, count, head_ref, tail_ref):
-    slots = ref.shape[-1]
+    size, slots = ref.shape[1], ref.shape[-1]
     lane = lax.broadcasted_iota(jnp.int32, (1, EDGE), 1)
     late = lane + (slots - EDGE) < count
+    at = 0
     for face in range(6):
         cells = plane(ref, face)
-        head_ref[face] = cells[..., :EDGE]
-        tail_ref[face] = jnp.where(
+        if face >= 2:
+            cells = cells[:, 1 : size - 1]
+        tiles = cells.shape[1]
+        head_ref[:, at : at + tiles] = cells[..., :EDGE]
+        tail_ref[:, at : at + tiles] = jnp.where(
             late, cells[..., slots - EDGE :], cells[..., slots - 2 * EDGE : slots - EDGE]
         )
-
-
-def edges_kernel(count_ref, u_ref, head_ref, tail_ref):
+        at += tiles
+
+
+def read_edges(ref, face):
+    size = ref.shape[2]
+    end = 0 if face % 2 == 0 else size - 1
+    if face < 2:
+        return ref[:, face * size : (face + 1) * size]
+    at = 2 * size + (face - 2) * (size - 2)
+    middle = ref[:, at : at + size - 2]
+    if face < 4:
+        first, last = ref[:, end : end + 1], ref[:, size + end : size + end + 1]
+    else:
+        first = ref[:, 0:size, end, :][:, None]
+        last = ref[:, size : 2 * size, end, :][:, None]
+    return jnp.concatenate([first, middle, last], axis=1)
+
+
+def edges_kernel(count_ref, u_ref, *refs):
+    head_ref, tail_ref = refs[-2:]
     write_edges(u_ref, count_ref[0], head_ref, tail_ref)
 
 
-def step_size(rates_ref, count_ref, var, slots):
-    live = lax.broadcasted_iota(jnp.int32, (1, slots), 1) < count_ref[0]
-    return jnp.where(live, rates_ref[var], 0.0)
-
-
-def local_kernel(base_ref, count_ref, rates_ref, near_ref, u_ref, out_ref, selector, ghosts):
+def step_body(start, base_ref, count_ref, rates_ref, near_ref, lower_ref, upper_ref, u_ref, out_ref, selector, ghosts):
     pair, size, _, _, slots = u_ref.shape
 
     @pl.when(pl.program_id(0) == 0)
     def _():
         for face in range(6):
-            index = relative(near_ref[face : face + 1, :], base_ref[0])
-            selector[face] = one_hot(index, slots)
+            index = near_ref[face : face + 1, :]
+            index = jnp.where(index < 0, FAR, index - base_ref[0])
+            index = jnp.where(
+                index < 0,
+                slots + (index & (EDGE - 1)),
+                jnp.where(index >= slots, index + EDGE, index),
+            )
+            selector[face] = one_hot(index, slots + 2 * EDGE)
 
     for face in range(6):
-        table = plane(u_ref, face ^ 1).reshape(pair * size * size, slots)
+        rows = pair * size * size
+        table = jnp.concatenate(
+            [
+                plane(u_ref, face ^ 1).reshape(rows, slots),
+                read_edges(lower_ref, face ^ 1).reshape(rows, EDGE),
+                read_edges(upper_ref, face ^ 1).reshape(rows, EDGE),
+            ],
+            axis=1,
+        )
         taken = picked(table, selector[face]).reshape(pair, size, size, slots)
         outer = near_ref[face : face + 1, :] < 0
         ghosts[face] = jnp.where(outer, plane(u_ref, face), taken)
@@ -90,7 +116,8 @@
     first, last = row == 0, row == size - 1
 
     def variable(v, carry):
-        factor = step_size(rates_ref, count_ref, pl.program_id(0) * pair + v, slots)
+        live = lax.broadcasted_iota(jnp.int32, (1, slots), 1) < count_ref[0]
+        factor = jnp.where(live, rates_ref[start + pl.program_id(0) * pair + v], 0.0)
         for i in range(size):
             for j in range(size):
                 cell = u_ref[v, i, j]
@@ -107,61 +134,27 @@
     lax.fori_loop(0, pair, variable, 0)
 
 
-def remote_body(base_ref, count_ref, rates_ref, near_ref, lower_ref, upper_ref, u_ref, out_ref, selector, ghosts):
-    pair, size, _, _, slots = u_ref.shape
+def edge_step_kernel(start, base_ref, count_ref, rates_ref, near_ref, lower_ref, upper_ref, u_ref, *refs):
+    out_ref, head_ref, tail_ref, selector, ghosts = refs[-5:]
+    step_body(start, base_ref, count_ref, rates_ref, near_ref, lower_ref, upper_ref, u_ref, out_ref, selector, ghosts)
+    write_edges(out_ref, count_ref[0], head_ref, tail_ref)
+
+
+def sum_step_kernel(start, base_ref, count_ref, rates_ref, near_ref, lower_ref, upper_ref, u_ref, *refs):
+    out_ref, sums_ref, selector, ghosts = refs[-4:]
+    step_body(start, base_ref, count_ref, rates_ref, near_ref, lower_ref, upper_ref, u_ref, out_ref, selector, ghosts)
+    for v in range(out_ref.shape[0]):
+        sums_ref[0, v : v + 1, :] = jnp.sum(jnp.sum(out_ref[v, 0], axis=0), axis=0, keepdims=True)
+
+
+def last_step_kernel(start, base_ref, count_ref, rates_ref, near_ref, lower_ref, upper_ref, u_ref, *refs):
+    added_ref = refs[0]
+    out_ref, selector, ghosts = refs[-3:]
+    step_body(start, base_ref, count_ref, rates_ref, near_ref, lower_ref, upper_ref, u_ref, out_ref, selector, ghosts)
 
     @pl.when(pl.program_id(0) == 0)
     def _():
-        for face in range(6):
-            index = relative(near_ref[face : face + 1, :], base_ref[0])
-            below = jnp.where(index < 0, index & (EDGE - 1), -1)
-            beyond = (index >= slots) & (index < FAR)
-            index = jnp.where(beyond, index - slots + EDGE, below)
-            selector[face] = one_hot(index, 2 * EDGE)
-
-    for face in range(6):
-        lower = lower_ref[face ^ 1].reshape(pair * size * size, EDGE)
-        upper = upper_ref[face ^ 1].reshape(pair * size * size, EDGE)
-        table = jnp.concatenate([lower, upper], axis=1)
-        ghosts[face] = picked(table, selector[face]).reshape(pair, size, size, slots)
-
-    row = lax.broadcasted_iota(jnp.int32, (size, slots), 0)
-    first, last = row == 0, row == size - 1
-
-    def variable(v, carry):
-        factor = step_size(rates_ref, count_ref, pl.program_id(0) * pair + v, slots)
-        for i in range(size):
-            for j in range(size):
-                extra = jnp.where(
-                    last,
-                    ghosts[5, v, i, j : j + 1, :],
-                    jnp.where(first, ghosts[4, v, i, j : j + 1, :], 0.0),
-                )
-                if i == 0:
-                    extra = extra + ghosts[0, v, j]
-                if i == size - 1:
-                    extra = extra + ghosts[1, v, j]
-                if j == 0:
-                    extra = extra + ghosts[2, v, i]
-                if j == size - 1:
-                    extra = extra + ghosts[3, v, i]
-                out_ref[v, i, j] = u_ref[v, i, j] + factor * extra
-        return carry
-
-    lax.fori_loop(0, pair, variable, 0)
-
-
-def remote_edges_kernel(base_ref, count_ref, rates_ref, near_ref, lower_ref, upper_ref, u_ref,
-                        out_ref, head_ref, tail_ref, selector, ghosts):
-    remote_body(base_ref, count_ref, rates_ref, near_ref, lower_ref, upper_ref, u_ref, out_ref, selector, ghosts)
-    write_edges(out_ref, count_ref[0], head_ref, tail_ref)
-
-
-def remote_sums_kernel(base_ref, count_ref, rates_ref, near_ref, lower_ref, upper_ref, u_ref,
-                       out_ref, sums_ref, selector, ghosts):
-    remote_body(base_ref, count_ref, rates_ref, near_ref, lower_ref, upper_ref, u_ref, out_ref, selector, ghosts)
-    for v in range(out_ref.shape[0]):
-        sums_ref[0, v : v + 1, :] = jnp.sum(jnp.sum(out_ref[v, 0], axis=0), axis=0, keepdims=True)
+        out_ref[1, 0] = out_ref[1, 0] + added_ref[...]
 
 
 def total(x):
@@ -189,7 +182,7 @@
 
     lax.fori_loop(1, devices, greet, 0)
     packet[0:1, :] = rows_ref[...].astype(F32)
-    packet[1:2, :] = (faces_ref[6:7, :] - faces_ref[5:6, :]) / 8.0
+    packet[1:2, :] = (faces_ref[2:3, :] - faces_ref[1:2, :]) / 8.0
     pl.semaphore_wait(barrier, devices - 1)
 
     def copy(step):
@@ -230,7 +223,7 @@
         whole_ref[b * lats : (b + 1) * lats, :] = slabs[b]
 
 
-def grid_kernel(shift, first_ref, parts_ref, cond_ref, rows_ref, u_ref, out_ref, share_ref, held):
+def grid_kernel(shift, first_ref, parts_ref, cond_ref, rows_ref, added_ref, share_ref, held):
     lats, lons = cond_ref.shape
     devices, _, slots = parts_ref.shape
     mask = lons - 1
@@ -278,8 +271,7 @@
     own = rows_ref[...]
     across = picked(potential, one_hot(jnp.where(own < 0, -1, own & mask), lons))
     here = lax.broadcasted_iota(jnp.int32, across.shape, 0) == (own >> shift)
-    added = jnp.sum(jnp.where(here, across, 0.0), axis=0, keepdims=True)
-    out_ref[...] = u_ref[...] + added
+    added_ref[...] = jnp.sum(jnp.where(here, across, 0.0), axis=0, keepdims=True)
 
 
 def smem():
@@ -294,62 +286,69 @@
     blk = lax.axis_index("blk")
     device = lax.axis_index("grp") * blks + blk
     base = jnp.reshape(device * slots, (1,)).astype(jnp.int32)
-    grid = (vars_ // PAIR,)
-    block = pl.BlockSpec((PAIR, size, size, size, slots), lambda g: (g, 0, 0, 0, 0))
-    edge = pl.BlockSpec((6, PAIR, size, size, EDGE), lambda g: (0, g, 0, 0, 0))
+    half = vars_ // 2
+    grid = (half // PAIR,)
+    tiles = 2 * size + 4 * (size - 2)
+    edge = pl.BlockSpec((PAIR, tiles, size, EDGE), lambda g: (g, 0, 0, 0))
     near = pl.BlockSpec(neighbours.shape, lambda g: (0, 0))
     sums = pl.BlockSpec((1, PAIR, slots), lambda g: (g, 0, 0))
+    anywhere = pl.BlockSpec(memory_space=pl.ANY)
     whole = jax.ShapeDtypeStruct(state.shape, F32)
-    edge_shape = jax.ShapeDtypeStruct((6, vars_, size, size, EDGE), F32)
-    sums_shape = jax.ShapeDtypeStruct((vars_ // PAIR, PAIR, slots), F32)
-    ghosts = pltpu.VMEM((6, PAIR, size, size, slots), F32)
+    part = jax.ShapeDtypeStruct((half,) + state.shape[1:], F32)
+    edge_shape = jax.ShapeDtypeStruct((half, tiles, size, EDGE), F32)
+    sums_shape = jax.ShapeDtypeStruct((half // PAIR, PAIR, slots), F32)
     up = [(d, d + 1) for d in range(devices - 1)]
     down = [(d + 1, d) for d in range(devices - 1)]
 
+    def block(start):
+        return pl.BlockSpec((PAIR, size, size, size, slots), lambda g: (g + start // PAIR, 0, 0, 0, 0))
+
     def exchange(head, tail):
         return lax.ppermute(tail, axes, up), lax.ppermute(head, axes, down)
 
-    def local(u):
+    def edges(start, *after):
         return pl.pallas_call(
-            local_kernel,
+            edges_kernel,
             grid=grid,
-            in_specs=[smem(), smem(), smem(), near, block],
-            out_specs=block,
-            out_shape=whole,
-            scratch_shapes=[pltpu.VMEM((6, slots, slots), BF16), ghosts],
+            in_specs=[smem(), block(start)] + [anywhere] * len(after),
+            out_specs=[edge, edge],
+            out_shape=[edge_shape, edge_shape],
             compiler_params=params(),
-            cost_estimate=pl.CostEstimate(flops=10 * 10**9, bytes_accessed=2 * u.size * 4, transcendentals=0),
-            name="local_step",
-        )(base, counts, rates, neighbours, u)
-
-    def remote(kernel, u, lower, upper, out_specs, out_shape):
+            cost_estimate=pl.CostEstimate(flops=10**6, bytes_accessed=8 * 10**6, transcendentals=0),
+            name="edges",
+        )(counts, state, *after)
+
+    def step(kernel, start, u, halo, out_specs, out_shape, extra=(), extra_specs=(), aliases={}):
         return pl.pallas_call(
-            kernel,
+            functools.partial(kernel, start),
             grid=grid,
-            in_specs=[smem(), smem(), smem(), near, edge, edge, block],
-            out_specs=[block] + out_specs,
-            out_shape=[whole] + out_shape,
-            scratch_shapes=[pltpu.VMEM((6, 2 * EDGE, slots), BF16), ghosts],
+            in_specs=[smem(), smem(), smem(), near, edge, edge, block(start if u is state else 0)]
+            + list(extra_specs),
+            out_specs=out_specs,
+            out_shape=out_shape,
+            scratch_shapes=[
+                pltpu.VMEM((6, slots + 2 * EDGE, slots), BF16),
+                pltpu.VMEM((6, PAIR, size, size, slots), F32),
+            ],
+            input_output_aliases=aliases,
             compiler_params=params(),
-            cost_estimate=pl.CostEstimate(flops=5 * 10**9, bytes_accessed=2 * u.size * 4, transcendentals=0),
-            name="remote_step",
-        )(base, counts, rates, neighbours, lower, upper, u)
-
-    head, tail = pl.pallas_call(
-        edges_kernel,
-        grid=grid,
-        in_specs=[smem(), block],
-        out_specs=[edge, edge],
-        out_shape=[edge_shape, edge_shape],
-        compiler_params=params(),
-        name="edges",
-    )(counts, state)
-    lower, upper = exchange(head, tail)
-    u = local(state)
-    u, head, tail = remote(remote_edges_kernel, u, lower, upper, [edge, edge], [edge_shape, edge_shape])
-    lower, upper = exchange(head, tail)
-    u = local(u)
-    u, faces = remote(remote_sums_kernel, u, lower, upper, [sums], [sums_shape])
+            cost_estimate=pl.CostEstimate(flops=5 * 10**9, bytes_accessed=30 * 10**6, transcendentals=0),
+            name="step",
+        )(base, counts, rates, neighbours, *halo, u, *extra)
+
+    head_b, tail_b = edges(half)
+    halo_b = exchange(head_b, tail_b)
+    head_a, tail_a = edges(0, head_b)
+    halo_a = exchange(head_a, tail_a)
+    outs = [block(0), edge, edge]
+    shapes = [part, edge_shape, edge_shape]
+    u_b, head_b, tail_b = step(edge_step_kernel, half, state, halo_b, outs, shapes)
+    halo_b = exchange(head_b, tail_b)
+    u_a, head_a, tail_a = step(edge_step_kernel, 0, state, halo_a, outs, shapes, (head_b,), (anywhere,))
+    halo_a = exchange(head_a, tail_a)
+    u, faces = step(
+        sum_step_kernel, half, u_b, halo_b, [block(half), sums], [whole, sums_shape], (head_a,), (anywhere,))
+
     lat_rows, lons = conductance.shape
     lats = lat_rows * blks
     own_rows = rows.reshape(1, slots)
@@ -370,31 +369,25 @@
         compiler_params=pltpu.CompilerParams(
             vmem_limit_bytes=VMEM_LIMIT, collective_id=0, has_side_effects=True),
         name="spread",
-    )(own_rows, faces.reshape(vars_, slots), conductance)
+    )(own_rows, faces.reshape(half, slots), conductance)
 
     first = jnp.reshape(blk * lat_rows, (1,)).astype(jnp.int32)
-    face = pl.BlockSpec((1, 1, size, size, slots), lambda g: (1, 0, 0, 0, 0))
 
     def full(*shape):
         return pl.BlockSpec(shape, lambda g: (0,) * len(shape))
 
-    u, share = pl.pallas_call(
+    added, share = pl.pallas_call(
         functools.partial(grid_kernel, lons.bit_length() - 1),
         grid=(1,),
-        in_specs=[
-            smem(),
-            full(devices, 2, slots),
-            full(lats, lons),
-            full(1, slots),
-            face,
-        ],
-        out_specs=[face, full(lat_rows, lons)],
-        out_shape=[whole, jax.ShapeDtypeStruct(conductance.shape, F32)],
+        in_specs=[smem(), full(devices, 2, slots), full(lats, lons), full(1, slots)],
+        out_specs=[full(1, slots), full(lat_rows, lons)],
+        out_shape=[jax.ShapeDtypeStruct((1, slots), F32), jax.ShapeDtypeStruct(conductance.shape, F32)],
         scratch_shapes=[pltpu.VMEM((lats, lons), F32)],
-        input_output_aliases={4: 0},
         compiler_params=params(),
+        cost_estimate=pl.CostEstimate(flops=5 * 10**9, bytes_accessed=10**6, transcendentals=0),
         name="ionosphere",
-    )(first, parts, conduct, own_rows, u)
+    )(first, parts, conduct, own_rows)
+    u = step(last_step_kernel, 0, u_a, halo_a, block(0), whole, (added, u), (full(1, slots), anywhere), {8: 0})
     return (u, share)
 
 

time: 123 us -> 95.7 us (0.78)
  Pallas kernels: 93.6 us -> 63.7 us
  starting transfers between devices: 27.7 us -> 30.1 us
    pallas_call x5 -> x6, Pallas kernels: 58.2 us -> 40.6 us  [the longest x4 35.1 us: step(): pl.pallas_call(functools.partial(kernel, start), grid=grid, in_specs=[sme...]
    pallas_call x1, Pallas kernels: 28.3 us -> 17 us  [on_device(): pl.pallas_call(functools.partial(spread_kernel, groups, blks), in_specs=[...]
    ppermute x4 -> x8, starting transfers between devices: 27.7 us -> 30.1 us  [exchange(): return (lax.ppermute(tail, axes, up), lax.ppermute(head, axes, down))]
  transfers between devices with their start and end apart: 4 -> 8, of which waited for: 0 -> 0; matrix products, arithmetic and copies ran while one was open for 0% -> 0% of each run, Pallas kernels for 27% -> 55%
where the time goes in v3:
time: 95.7 us; the launch traced here: 95.4 us
  Pallas kernels  63.7 us (67%)
  starting transfers between devices  30.1 us (31%)
  between operations  1.49 us (2%)
    pallas_call x4, Pallas kernels, step(): pl.pallas_call(functools.partial(kernel, start), grid=grid, in_specs=[sme...  35.1 us
    ppermute x8, starting transfers between devices, exchange(): return (lax.ppermute(tail, axes, up), lax.ppermute(head, axes, down))  30.1 us
    pallas_call x1, Pallas kernels, on_device(): pl.pallas_call(functools.partial(spread_kernel, groups, blks), in_specs=[...  17 us
    pallas_call x1, Pallas kernels, on_device(): pl.pallas_call(functools.partial(grid_kernel, lons.bit_length() - 1), gri...  6.06 us
    pallas_call x2, Pallas kernels, edges(): pl.pallas_call(edges_kernel, grid=grid, in_specs=[smem(), block(start)] +...  5.5 us
  transfers between devices with their start and end apart: 8, of which 0 were waited for; matrix products, arithmetic and copies ran while one was open for 0% of the time, Pallas kernels for 55%

profile of v3, /device:TPU:0, one launch (start us, length us, event | category | flops | bytes accessed | tf_op | source)
XLA Modules:
  0.0 95.4 jit_solution(14421423423604855963)
XLA Ops:
  1.3 3.1 %edges.2 = (f32[4,40,8,128]{3,2,1,0:T(8,128)S(1)}, f32[4,40,8,128]{3,2,1,0:T(8,128)}) custom-call(s32[1]{0:T(128)S(6)} %copy.10.count_ref, f32[8,8,8,8,512]{4,3,2,1,0:T(8,128)} %u_ref.7), custom_call_target="tpu_custom_call" | custom-call | flops 1000000 | bytes 8000000 | tf_op jit(solution)/shard_map/edges/pallas_call | solution.py:310
  4.4 3.2 %collective-permute-start.2 = (f32[4,40,8,128]{3,2,1,0:T(8,128)}, f32[4,40,8,128]{3,2,1,0:T(8,128)}, u32[]{:S(2)}, u32[]{:S(2)}) collective-permute-start(f32[4,40,8,128]{3,2,1,0:T(8,128)} %get-tuple-element.21), channel_id=1, source_target_pairs={{0,1},{1,2},{2,3},{3,4},{4,5},{5,6},{6,7},{7,8},{8,9},{9,10},{10,1... | collective-permute-start | bytes 1966088 | tf_op jit(solution)/shard_map/ppermute | solution.py:307
  7.6 1.3 %collective-permute-start.3 = (f32[4,40,8,128]{3,2,1,0:T(8,128)S(1)}, f32[4,40,8,128]{3,2,1,0:T(8,128)}, u32[]{:S(2)}, u32[]{:S(2)}) collective-permute-start(f32[4,40,8,128]{3,2,1,0:T(8,128)S(1)} %get-tuple-element.18.refs_0_), channel_id=1, source_target_pairs={{1,0},{2,1},{3,2},{4,3},{5,4},{6,5},{7,6},{8,7},{9,8},{10,9},{11,1... | collective-permute-start | bytes 1966088 | tf_op jit(solution)/shard_map/ppermute | solution.py:307
  8.9 2.4 %edges.3 = (f32[4,40,8,128]{3,2,1,0:T(8,128)S(1)}, f32[4,40,8,128]{3,2,1,0:T(8,128)S(1)}) custom-call(s32[1]{0:T(128)S(6)} %copy.10.count_ref, f32[8,8,8,8,512]{4,3,2,1,0:T(8,128)} %u_ref.7, f32[4,40,8,128]{3,2,1,0:T(8,128)S(1)} %get-tuple-element.18.refs_0_), custom_call_target="tpu_custom_call" | custom-call | flops 1000000 | bytes 8000000 | tf_op jit(solution)/shard_map/edges/pallas_call | solution.py:310
  11.3 4.3 %collective-permute-start = (f32[4,40,8,128]{3,2,1,0:T(8,128)S(1)}, f32[4,40,8,128]{3,2,1,0:T(8,128)S(1)}, u32[]{:S(2)}, u32[]{:S(2)}) collective-permute-start(f32[4,40,8,128]{3,2,1,0:T(8,128)S(1)} %get-tuple-element.19), channel_id=1, source_target_pairs={{0,1},{1,2},{2,3},{3,4},{4,5},{5,6},{6,7},{7,8},{8,9},{9,10},{10,1... | collective-permute-start | bytes 1966088 | tf_op jit(solution)/shard_map/ppermute | solution.py:307
  15.7 1.3 %collective-permute-start.1 = (f32[4,40,8,128]{3,2,1,0:T(8,128)S(1)}, f32[4,40,8,128]{3,2,1,0:T(8,128)S(1)}, u32[]{:S(2)}, u32[]{:S(2)}) collective-permute-start(f32[4,40,8,128]{3,2,1,0:T(8,128)S(1)} %get-tuple-element.20), channel_id=1, source_target_pairs={{1,0},{2,1},{3,2},{4,3},{5,4},{6,5},{7,6},{8,7},{9,8},{10,9},{11,1... | collective-permute-start | bytes 1966088 | tf_op jit(solution)/shard_map/ppermute | solution.py:307
  17.0 0.0 collective-permute-done.2.lower_ref
  17.0 0.0 collective-permute-done.3.upper_ref
  17.0 9.5 %step.4 = (f32[4,8,8,8,512]{4,3,2,1,0:T(8,128)}, f32[4,40,8,128]{3,2,1,0:T(8,128)}, f32[4,40,8,128]{3,2,1,0:T(8,128)}) custom-call(s32[1]{0:T(128)} %bitcast.base_ref, s32[1]{0:T(128)S(6)} %copy.10.count_ref, f32[8]{0:T(128)S(1)} %copy-done.4, s32[6,512]{1,0:T(8,128)S(1)} %copy-done.1, f32[4,40,8,128]{3,2,1,0:T(8,128)} %collective-permute-done.2.lower_ref, ...), custom_call_target="tpu_custom_call" | custom-call | flops 5000000000 | bytes 30000000 | tf_op jit(solution)/shard_map/step/pallas_call | solution.py:322
  26.5 14.2 %collective-permute-start.6 = (f32[4,40,8,128]{3,2,1,0:T(8,128)}, f32[4,40,8,128]{3,2,1,0:T(8,128)}, u32[]{:S(2)}, u32[]{:S(2)}) collective-permute-start(f32[4,40,8,128]{3,2,1,0:T(8,128)} %get-tuple-element.26), channel_id=1, source_target_pairs={{0,1},{1,2},{2,3},{3,4},{4,5},{5,6},{6,7},{7,8},{8,9},{9,10},{10,1... | collective-permute-start | bytes 1966088 | tf_op jit(solution)/shard_map/ppermute | solution.py:307
  40.7 1.3 %collective-permute-start.7 = (f32[4,40,8,128]{3,2,1,0:T(8,128)}, f32[4,40,8,128]{3,2,1,0:T(8,128)}, u32[]{:S(2)}, u32[]{:S(2)}) collective-permute-start(f32[4,40,8,128]{3,2,1,0:T(8,128)} %get-tuple-element.22.refs_0_), channel_id=1, source_target_pairs={{1,0},{2,1},{3,2},{4,3},{5,4},{6,5},{7,6},{8,7},{9,8},{10,9},{11,1... | collective-permute-start | bytes 1966088 | tf_op jit(solution)/shard_map/ppermute | solution.py:307
  42.0 0.0 copy-start.5
  42.0 0.0 collective-permute-done.lower_ref
  42.0 9.0 %step.5 = (f32[4,8,8,8,512]{4,3,2,1,0:T(8,128)}, f32[4,40,8,128]{3,2,1,0:T(8,128)S(1)}, f32[4,40,8,128]{3,2,1,0:T(8,128)S(1)}) custom-call(s32[1]{0:T(128)} %bitcast.base_ref, s32[1]{0:T(128)S(6)} %copy.10.count_ref, f32[8]{0:T(128)S(1)} %copy-done.4, s32[6,512]{1,0:T(8,128)S(1)} %copy-done.1, f32[4,40,8,128]{3,2,1,0:T(8,128)S(1)} %collective-permute-done.lower_ref, ...), custom_call_target="tpu_custom_call" | custom-call | flops 5000000000 | bytes 30000000 | tf_op jit(solution)/shard_map/step/pallas_call | solution.py:322
  51.0 3.1 %collective-permute-start.4 = (f32[4,40,8,128]{3,2,1,0:T(8,128)S(1)}, f32[4,40,8,128]{3,2,1,0:T(8,128)S(1)}, u32[]{:S(2)}, u32[]{:S(2)}) collective-permute-start(f32[4,40,8,128]{3,2,1,0:T(8,128)S(1)} %get-tuple-element.23), channel_id=1, source_target_pairs={{0,1},{1,2},{2,3},{3,4},{4,5},{5,6},{6,7},{7,8},{8,9},{9,10},{10,1... | collective-permute-start | bytes 1966088 | tf_op jit(solution)/shard_map/ppermute | solution.py:307
  54.1 1.5 %collective-permute-start.5 = (f32[4,40,8,128]{3,2,1,0:T(8,128)S(1)}, f32[4,40,8,128]{3,2,1,0:T(8,128)S(1)}, u32[]{:S(2)}, u32[]{:S(2)}) collective-permute-start(f32[4,40,8,128]{3,2,1,0:T(8,128)S(1)} %get-tuple-element.24.refs_0_), channel_id=1, source_target_pairs={{1,0},{2,1},{3,2},{4,3},{5,4},{6,5},{7,6},{8,7},{9,8},{10,9},{11,1... | collective-permute-start | bytes 1966088 | tf_op jit(solution)/shard_map/ppermute | solution.py:307
  55.6 0.0 collective-permute-done.7.upper_ref
  55.6 0.0 copy-start.2
  55.6 0.0 copy-start.3
  55.6 8.3 %step.6 = (f32[8,8,8,8,512]{4,3,2,1,0:T(8,128)}, f32[2,2,512]{2,1,0:T(2,128)S(1)}) custom-call(s32[1]{0:T(128)} %bitcast.base_ref, s32[1]{0:T(128)S(6)} %copy.10.count_ref, f32[8]{0:T(128)S(1)} %copy-done.4, s32[6,512]{1,0:T(8,128)S(1)} %copy-done.1, f32[4,40,8,128]{3,2,1,0:T(8,128)} %collective-permute-done.6.lower_ref, ...), custom_call_target="tpu_custom_call" | custom-call | flops 5000000000 | bytes 30000000 | tf_op jit(solution)/shard_map/step/pallas_call | solution.py:322
  63.9 17.0 %spread.1 = (f32[32,2,512]{2,1,0:T(2,128)S(1)}, f32[96,256]{1,0:T(8,128)S(1)}) custom-call(s32[1,512]{1,0:T(1,128)S(1)} %bitcast.3, f32[4,512]{1,0:T(4,128)S(1)} %reshape.19.faces_ref, f32[12,256]{1,0:T(8,128)S(1)} %copy-done.2), custom_call_target="tpu_custom_call" | custom-call | tf_op jit(solution)/shard_map/spread/pallas_call | solution.py:355
  80.9 6.1 %ionosphere.1 = (f32[1,512]{1,0:T(1,128)S(1)}, f32[12,256]{1,0:T(8,128)}) custom-call(s32[1]{0:T(128)} %bitcast.1.first_ref, f32[32,2,512]{2,1,0:T(2,128)S(1)} %get-tuple-element.29.parts_ref, f32[96,256]{1,0:T(8,128)S(1)} %get-tuple-element.30.cond_ref, s32[1,512]{1,0:T(1,128)S(1)} %bitcast.4), custom_call_target="tpu_custom_call" | custom-call | flops 5000000000 | bytes 1000000 | tf_op jit(solution)/shard_map/ionosphere/pallas_call | solution.py:379
  87.0 0.0 collective-permute-done.5.upper_ref
  87.0 8.4 %step.7 = f32[8,8,8,8,512]{4,3,2,1,0:T(8,128)} custom-call(s32[1]{0:T(128)} %bitcast.base_ref, s32[1]{0:T(128)S(6)} %copy.10.count_ref, f32[8]{0:T(128)S(1)} %copy-done.4, s32[6,512]{1,0:T(8,128)S(1)} %copy-done.1, f32[4,40,8,128]{3,2,1,0:T(8,128)S(1)} %collective-permute-done.4.lower_ref, ...), custom_call_target="tpu_custom_call", output_to_operand_aliasing={{}: (8, {})} | custom-call | flops 5000000000 | bytes 30000000 | tf_op jit(solution)/shard_map/step/pallas_call | solution.py:322
  (13 shorter events, 0.0 us)
Async XLA Ops:
  1.3 15.7 %copy-start.1 = (s32[6,512]{1,0:T(8,128)S(1)}, s32[6,512]{1,0:T(8,128)}, u32[]{:S(2)}) copy-start(s32[6,512]{1,0:T(8,128)} %near_ref.7) | copy-start | bytes 36868
  1.3 15.7 %copy-start.4 = (f32[8]{0:T(128)S(1)}, f32[8]{0:T(128)}, u32[]{:S(2)}) copy-start(f32[8]{0:T(128)} %rates_ref.7) | copy-start | bytes 100
  4.4 12.5 %collective-permute-start.2 = (f32[4,40,8,128]{3,2,1,0:T(8,128)}, f32[4,40,8,128]{3,2,1,0:T(8,128)}, u32[]{:S(2)}, u32[]{:S(2)}) collective-permute-start(f32[4,40,8,128]{3,2,1,0:T(8,128)} %get-tuple-element.21), channel_id=1, source_target_pairs={{0,1},{1,2},{2,3},{3,4},{4,5},{5,6},{6,7},{7,8},{8,9},{9,10},{10,1... | collective-permute-start | bytes 1966088 | tf_op jit(solution)/shard_map/ppermute | solution.py:307
  7.6 9.4 %collective-permute-start.3 = (f32[4,40,8,128]{3,2,1,0:T(8,128)S(1)}, f32[4,40,8,128]{3,2,1,0:T(8,128)}, u32[]{:S(2)}, u32[]{:S(2)}) collective-permute-start(f32[4,40,8,128]{3,2,1,0:T(8,128)S(1)} %get-tuple-element.18.refs_0_), channel_id=1, source_target_pairs={{1,0},{2,1},{3,2},{4,3},{5,4},{6,5},{7,6},{8,7},{9,8},{10,9},{11,1... | collective-permute-start | bytes 1966088 | tf_op jit(solution)/shard_map/ppermute | solution.py:307
  11.3 30.7 %collective-permute-start = (f32[4,40,8,128]{3,2,1,0:T(8,128)S(1)}, f32[4,40,8,128]{3,2,1,0:T(8,128)S(1)}, u32[]{:S(2)}, u32[]{:S(2)}) collective-permute-start(f32[4,40,8,128]{3,2,1,0:T(8,128)S(1)} %get-tuple-element.19), channel_id=1, source_target_pairs={{0,1},{1,2},{2,3},{3,4},{4,5},{5,6},{6,7},{7,8},{8,9},{9,10},{10,1... | collective-permute-start | bytes 1966088 | tf_op jit(solution)/shard_map/ppermute | solution.py:307
  15.7 26.4 %collective-permute-start.1 = (f32[4,40,8,128]{3,2,1,0:T(8,128)S(1)}, f32[4,40,8,128]{3,2,1,0:T(8,128)S(1)}, u32[]{:S(2)}, u32[]{:S(2)}) collective-permute-start(f32[4,40,8,128]{3,2,1,0:T(8,128)S(1)} %get-tuple-element.20), channel_id=1, source_target_pairs={{1,0},{2,1},{3,2},{4,3},{5,4},{6,5},{7,6},{8,7},{9,8},{10,9},{11,1... | collective-permute-start | bytes 1966088 | tf_op jit(solution)/shard_map/ppermute | solution.py:307
  26.5 29.0 %collective-permute-start.6 = (f32[4,40,8,128]{3,2,1,0:T(8,128)}, f32[4,40,8,128]{3,2,1,0:T(8,128)}, u32[]{:S(2)}, u32[]{:S(2)}) collective-permute-start(f32[4,40,8,128]{3,2,1,0:T(8,128)} %get-tuple-element.26), channel_id=1, source_target_pairs={{0,1},{1,2},{2,3},{3,4},{4,5},{5,6},{6,7},{7,8},{8,9},{9,10},{10,1... | collective-permute-start | bytes 1966088 | tf_op jit(solution)/shard_map/ppermute | solution.py:307
  40.7 14.9 %collective-permute-start.7 = (f32[4,40,8,128]{3,2,1,0:T(8,128)}, f32[4,40,8,128]{3,2,1,0:T(8,128)}, u32[]{:S(2)}, u32[]{:S(2)}) collective-permute-start(f32[4,40,8,128]{3,2,1,0:T(8,128)} %get-tuple-element.22.refs_0_), channel_id=1, source_target_pairs={{1,0},{2,1},{3,2},{4,3},{5,4},{6,5},{7,6},{8,7},{9,8},{10,9},{11,1... | collective-permute-start | bytes 1966088 | tf_op jit(solution)/shard_map/ppermute | solution.py:307
  42.0 13.6 %copy-start.5 = (f32[4,8,8,8,512]{4,3,2,1,0:T(8,128)S(1)}, f32[4,8,8,8,512]{4,3,2,1,0:T(8,128)}, u32[]{:S(2)}) copy-start(f32[4,8,8,8,512]{4,3,2,1,0:T(8,128)} %get-tuple-element.27.u_ref) | copy-start | bytes 12582916
  51.0 36.0 %collective-permute-start.4 = (f32[4,40,8,128]{3,2,1,0:T(8,128)S(1)}, f32[4,40,8,128]{3,2,1,0:T(8,128)S(1)}, u32[]{:S(2)}, u32[]{:S(2)}) collective-permute-start(f32[4,40,8,128]{3,2,1,0:T(8,128)S(1)} %get-tuple-element.23), channel_id=1, source_target_pairs={{0,1},{1,2},{2,3},{3,4},{4,5},{5,6},{6,7},{7,8},{8,9},{9,10},{10,1... | collective-permute-start | bytes 1966088 | tf_op jit(solution)/shard_map/ppermute | solution.py:307
  54.1 32.9 %collective-permute-start.5 = (f32[4,40,8,128]{3,2,1,0:T(8,128)S(1)}, f32[4,40,8,128]{3,2,1,0:T(8,128)S(1)}, u32[]{:S(2)}, u32[]{:S(2)}) collective-permute-start(f32[4,40,8,128]{3,2,1,0:T(8,128)S(1)} %get-tuple-element.24.refs_0_), channel_id=1, source_target_pairs={{1,0},{2,1},{3,2},{4,3},{5,4},{6,5},{7,6},{8,7},{9,8},{10,9},{11,1... | collective-permute-start | bytes 1966088 | tf_op jit(solution)/shard_map/ppermute | solution.py:307
  55.6 8.3 %copy-start.2 = (f32[12,256]{1,0:T(8,128)S(1)}, f32[12,256]{1,0:T(8,128)}, u32[]{:S(2)}) copy-start(f32[12,256]{1,0:T(8,128)} %cond_ref.1) | copy-start | bytes 36868
  55.6 8.3 %copy-start.3 = (s32[512]{0:T(512)S(1)}, s32[512]{0:T(512)}, u32[]{:S(2)}) copy-start(s32[512]{0:T(512)} %param.9) | copy-start | bytes 6148
  80.9 6.1 %copy-start = (f32[4,8,8,8,512]{4,3,2,1,0:T(8,128)S(1)}, f32[4,8,8,8,512]{4,3,2,1,0:T(8,128)}, u32[]{:S(2)}) copy-start(f32[4,8,8,8,512]{4,3,2,1,0:T(8,128)} %get-tuple-element.25.u_ref) | copy-start | bytes 12582916

commit v4 on v3

--- a/solution.py
+++ b/solution.py
@@ -98,11 +98,12 @@
             )
             selector[face] = one_hot(index, slots + 2 * EDGE)
 
+    own = [plane(u_ref, face) for face in range(6)]
     for face in range(6):
         rows = pair * size * size
         table = jnp.concatenate(
             [
-                plane(u_ref, face ^ 1).reshape(rows, slots),
+                own[face ^ 1].reshape(rows, slots),
                 read_edges(lower_ref, face ^ 1).reshape(rows, EDGE),
                 read_edges(upper_ref, face ^ 1).reshape(rows, EDGE),
             ],
@@ -110,7 +111,7 @@
         )
         taken = picked(table, selector[face]).reshape(pair, size, size, slots)
         outer = near_ref[face : face + 1, :] < 0
-        ghosts[face] = jnp.where(outer, plane(u_ref, face), taken)
+        ghosts[face] = jnp.where(outer, own[face], taken)
 
     row = lax.broadcasted_iota(jnp.int32, (size, slots), 0)
     first, last = row == 0, row == size - 1
@@ -339,6 +340,7 @@
     head_b, tail_b = edges(half)
     halo_b = exchange(head_b, tail_b)
     head_a, tail_a = edges(0, head_b)
+    head_a, tail_a, *halo_b = lax.optimization_barrier((head_a, tail_a, *halo_b))
     halo_a = exchange(head_a, tail_a)
     outs = [block(0), edge, edge]
     shapes = [part, edge_shape, edge_shape]

time: 95.7 us -> 94.3 us (0.985)
  Pallas kernels: 63.7 us -> 60.9 us
  waiting for transfers between devices: 0.02 us -> 1.5 us
    pallas_call x1, Pallas kernels: 17 us -> 15 us  [on_device(): pl.pallas_call(functools.partial(spread_kernel, groups, blks), in_specs=[...]
    ppermute x8, waiting for transfers between devices: 0.02 us -> 1.5 us  [exchange(): return (lax.ppermute(tail, axes, up), lax.ppermute(head, axes, down))]
  transfers between devices with their start and end apart: 8 -> 8, of which waited for: 0 -> 1; matrix products, arithmetic and copies ran while one was open for 0% -> 0% of each run, Pallas kernels for 55% -> 54%
where the time goes in v4:
time: 94.3 us; the launch traced here: 93.9 us
  Pallas kernels  60.9 us (65%)
  starting transfers between devices  30 us (32%)
  waiting for transfers between devices  1.5 us (2%)
  between operations  1.49 us (2%)
    pallas_call x4, Pallas kernels, step(): pl.pallas_call(functools.partial(kernel, start), grid=grid, in_specs=[sme...  34.2 us
    ppermute x8, starting transfers between devices, exchange(): return (lax.ppermute(tail, axes, up), lax.ppermute(head, axes, down))  30 us
    pallas_call x1, Pallas kernels, on_device(): pl.pallas_call(functools.partial(spread_kernel, groups, blks), in_specs=[...  15 us
    pallas_call x1, Pallas kernels, on_device(): pl.pallas_call(functools.partial(grid_kernel, lons.bit_length() - 1), gri...  6.06 us
    pallas_call x2, Pallas kernels, edges(): pl.pallas_call(edges_kernel, grid=grid, in_specs=[smem(), block(start)] +...  5.65 us
  transfers between devices with their start and end apart: 8, of which 1 were waited for; matrix products, arithmetic and copies ran while one was open for 0% of the time, Pallas kernels for 54%

profile of v4, /device:TPU:0, one launch (start us, length us, event | category | flops | bytes accessed | tf_op | source)
XLA Modules:
  0.0 93.9 jit_solution(4819821575432368)
XLA Ops:
  1.3 2.4 %edges.2 = (f32[4,40,8,128]{3,2,1,0:T(8,128)S(1)}, f32[4,40,8,128]{3,2,1,0:T(8,128)S(1)}) custom-call(s32[1]{0:T(128)S(6)} %copy.10.count_ref, f32[8,8,8,8,512]{4,3,2,1,0:T(8,128)} %u_ref.7), custom_call_target="tpu_custom_call" | custom-call | flops 1000000 | bytes 8000000 | tf_op jit(solution)/shard_map/edges/pallas_call | solution.py:311
  3.7 2.4 %collective-permute-start = (f32[4,40,8,128]{3,2,1,0:T(8,128)S(1)}, f32[4,40,8,128]{3,2,1,0:T(8,128)S(1)}, u32[]{:S(2)}, u32[]{:S(2)}) collective-permute-start(f32[4,40,8,128]{3,2,1,0:T(8,128)S(1)} %get-tuple-element.25), channel_id=1, source_target_pairs={{0,1},{1,2},{2,3},{3,4},{4,5},{5,6},{6,7},{7,8},{8,9},{9,10},{10,1... | collective-permute-start | bytes 1966088 | tf_op jit(solution)/shard_map/ppermute | solution.py:308
  6.1 1.3 %collective-permute-start.1 = (f32[4,40,8,128]{3,2,1,0:T(8,128)S(1)}, f32[4,40,8,128]{3,2,1,0:T(8,128)S(1)}, u32[]{:S(2)}, u32[]{:S(2)}) collective-permute-start(f32[4,40,8,128]{3,2,1,0:T(8,128)S(1)} %get-tuple-element.22.refs_0_), channel_id=1, source_target_pairs={{1,0},{2,1},{3,2},{4,3},{5,4},{6,5},{7,6},{8,7},{9,8},{10,9},{11,1... | collective-permute-start | bytes 1966088 | tf_op jit(solution)/shard_map/ppermute | solution.py:308
  7.4 3.3 %edges.3 = (f32[4,40,8,128]{3,2,1,0:T(8,128)}, f32[4,40,8,128]{3,2,1,0:T(8,128)}) custom-call(s32[1]{0:T(128)S(6)} %copy.10.count_ref, f32[8,8,8,8,512]{4,3,2,1,0:T(8,128)} %u_ref.7, f32[4,40,8,128]{3,2,1,0:T(8,128)S(1)} %get-tuple-element.22.refs_0_), custom_call_target="tpu_custom_call" | custom-call | flops 1000000 | bytes 8000000 | tf_op jit(solution)/shard_map/edges/pallas_call | solution.py:311
  10.7 0.0 collective-permute-done.lower_ref
  10.7 1.5 %collective-permute-done.1.upper_ref = f32[4,40,8,128]{3,2,1,0:T(8,128)S(1)} collective-permute-done((f32[4,40,8,128]{3,2,1,0:T(8,128)S(1)}, f32[4,40,8,128]{3,2,1,0:T(8,128)S(1)}, u32[]{:S(2)}, u32[]{:S(2)}) %collective-permute-start.1) | collective-permute-done | bytes 655392 | tf_op jit(solution)/shard_map/ppermute | solution.py:308
  12.2 14.6 %collective-permute-start.2 = (f32[4,40,8,128]{3,2,1,0:T(8,128)}, f32[4,40,8,128]{3,2,1,0:T(8,128)S(1)}, u32[]{:S(2)}, u32[]{:S(2)}) collective-permute-start(f32[4,40,8,128]{3,2,1,0:T(8,128)} %get-tuple-element.26), channel_id=1, source_target_pairs={{0,1},{1,2},{2,3},{3,4},{4,5},{5,6},{6,7},{7,8},{8,9},{9,10},{10,1... | collective-permute-start | bytes 1966088 | tf_op jit(solution)/shard_map/ppermute | solution.py:308
  26.8 1.3 %collective-permute-start.3 = (f32[4,40,8,128]{3,2,1,0:T(8,128)}, f32[4,40,8,128]{3,2,1,0:T(8,128)}, u32[]{:S(2)}, u32[]{:S(2)}) collective-permute-start(f32[4,40,8,128]{3,2,1,0:T(8,128)} %get-tuple-element.27), channel_id=1, source_target_pairs={{1,0},{2,1},{3,2},{4,3},{5,4},{6,5},{7,6},{8,7},{9,8},{10,9},{11,1... | collective-permute-start | bytes 1966088 | tf_op jit(solution)/shard_map/ppermute | solution.py:308
  28.1 8.8 %step.4 = (f32[4,8,8,8,512]{4,3,2,1,0:T(8,128)}, f32[4,40,8,128]{3,2,1,0:T(8,128)S(1)}, f32[4,40,8,128]{3,2,1,0:T(8,128)}) custom-call(s32[1]{0:T(128)} %bitcast.base_ref, s32[1]{0:T(128)S(6)} %copy.10.count_ref, f32[8]{0:T(128)S(1)} %copy-done.4, s32[6,512]{1,0:T(8,128)S(1)} %copy-done.1, f32[4,40,8,128]{3,2,1,0:T(8,128)S(1)} %collective-permute-done.lower_ref, ...), custom_call_target="tpu_custom_call" | custom-call | flops 5000000000 | bytes 30000000 | tf_op jit(solution)/shard_map/step/pallas_call | solution.py:323
  37.0 3.4 %collective-permute-start.6 = (f32[4,40,8,128]{3,2,1,0:T(8,128)}, f32[4,40,8,128]{3,2,1,0:T(8,128)S(1)}, u32[]{:S(2)}, u32[]{:S(2)}) collective-permute-start(f32[4,40,8,128]{3,2,1,0:T(8,128)} %get-tuple-element.34), channel_id=1, source_target_pairs={{0,1},{1,2},{2,3},{3,4},{4,5},{5,6},{6,7},{7,8},{8,9},{9,10},{10,1... | collective-permute-start | bytes 1966088 | tf_op jit(solution)/shard_map/ppermute | solution.py:308
  40.3 1.3 %collective-permute-start.7 = (f32[4,40,8,128]{3,2,1,0:T(8,128)S(1)}, f32[4,40,8,128]{3,2,1,0:T(8,128)}, u32[]{:S(2)}, u32[]{:S(2)}) collective-permute-start(f32[4,40,8,128]{3,2,1,0:T(8,128)S(1)} %get-tuple-element.30.refs_0_), channel_id=1, source_target_pairs={{1,0},{2,1},{3,2},{4,3},{5,4},{6,5},{7,6},{8,7},{9,8},{10,9},{11,1... | collective-permute-start | bytes 1966088 | tf_op jit(solution)/shard_map/ppermute | solution.py:308
  41.6 0.0 copy-start.5
  41.6 0.0 collective-permute-done.2.lower_ref
  41.6 0.0 collective-permute-done.3.upper_ref
  41.7 9.1 %step.5 = (f32[4,8,8,8,512]{4,3,2,1,0:T(8,128)}, f32[4,40,8,128]{3,2,1,0:T(8,128)S(1)}, f32[4,40,8,128]{3,2,1,0:T(8,128)}) custom-call(s32[1]{0:T(128)} %bitcast.base_ref, s32[1]{0:T(128)S(6)} %copy.10.count_ref, f32[8]{0:T(128)S(1)} %copy-done.4, s32[6,512]{1,0:T(8,128)S(1)} %copy-done.1, f32[4,40,8,128]{3,2,1,0:T(8,128)S(1)} %collective-permute-done.2.lower_ref, ...), custom_call_target="tpu_custom_call" | custom-call | flops 5000000000 | bytes 30000000 | tf_op jit(solution)/shard_map/step/pallas_call | solution.py:323
  50.8 4.3 %collective-permute-start.4 = (f32[4,40,8,128]{3,2,1,0:T(8,128)}, f32[4,40,8,128]{3,2,1,0:T(8,128)S(1)}, u32[]{:S(2)}, u32[]{:S(2)}) collective-permute-start(f32[4,40,8,128]{3,2,1,0:T(8,128)} %get-tuple-element.31), channel_id=1, source_target_pairs={{0,1},{1,2},{2,3},{3,4},{4,5},{5,6},{6,7},{7,8},{8,9},{9,10},{10,1... | collective-permute-start | bytes 1966088 | tf_op jit(solution)/shard_map/ppermute | solution.py:308
  55.0 1.5 %collective-permute-start.5 = (f32[4,40,8,128]{3,2,1,0:T(8,128)S(1)}, f32[4,40,8,128]{3,2,1,0:T(8,128)S(1)}, u32[]{:S(2)}, u32[]{:S(2)}) collective-permute-start(f32[4,40,8,128]{3,2,1,0:T(8,128)S(1)} %get-tuple-element.32.refs_0_), channel_id=1, source_target_pairs={{1,0},{2,1},{3,2},{4,3},{5,4},{6,5},{7,6},{8,7},{9,8},{10,9},{11,1... | collective-permute-start | bytes 1966088 | tf_op jit(solution)/shard_map/ppermute | solution.py:308
  56.5 0.0 collective-permute-done.6.lower_ref
  56.5 0.0 copy-start.2
  56.5 0.0 copy-start.3
  56.6 8.0 %step.6 = (f32[8,8,8,8,512]{4,3,2,1,0:T(8,128)}, f32[2,2,512]{2,1,0:T(2,128)S(1)}) custom-call(s32[1]{0:T(128)} %bitcast.base_ref, s32[1]{0:T(128)S(6)} %copy.10.count_ref, f32[8]{0:T(128)S(1)} %copy-done.4, s32[6,512]{1,0:T(8,128)S(1)} %copy-done.1, f32[4,40,8,128]{3,2,1,0:T(8,128)S(1)} %collective-permute-done.6.lower_ref, ...), custom_call_target="tpu_custom_call" | custom-call | flops 5000000000 | bytes 30000000 | tf_op jit(solution)/shard_map/step/pallas_call | solution.py:323
  64.6 15.0 %spread.1 = (f32[32,2,512]{2,1,0:T(2,128)S(1)}, f32[96,256]{1,0:T(8,128)S(1)}) custom-call(s32[1,512]{1,0:T(1,128)S(1)} %bitcast.3, f32[4,512]{1,0:T(4,128)S(1)} %reshape.19.faces_ref, f32[12,256]{1,0:T(8,128)S(1)} %copy-done.2), custom_call_target="tpu_custom_call" | custom-call | tf_op jit(solution)/shard_map/spread/pallas_call | solution.py:357
  79.7 6.1 %ionosphere.1 = (f32[1,512]{1,0:T(1,128)S(1)}, f32[12,256]{1,0:T(8,128)}) custom-call(s32[1]{0:T(128)} %bitcast.1.first_ref, f32[32,2,512]{2,1,0:T(2,128)S(1)} %get-tuple-element.37.parts_ref, f32[96,256]{1,0:T(8,128)S(1)} %get-tuple-element.38.cond_ref, s32[1,512]{1,0:T(1,128)S(1)} %bitcast.4), custom_call_target="tpu_custom_call" | custom-call | flops 5000000000 | bytes 1000000 | tf_op jit(solution)/shard_map/ionosphere/pallas_call | solution.py:381
  85.8 8.2 %step.7 = f32[8,8,8,8,512]{4,3,2,1,0:T(8,128)} custom-call(s32[1]{0:T(128)} %bitcast.base_ref, s32[1]{0:T(128)S(6)} %copy.10.count_ref, f32[8]{0:T(128)S(1)} %copy-done.4, s32[6,512]{1,0:T(8,128)S(1)} %copy-done.1, f32[4,40,8,128]{3,2,1,0:T(8,128)S(1)} %collective-permute-done.4.lower_ref, ...), custom_call_target="tpu_custom_call", output_to_operand_aliasing={{}: (8, {})} | custom-call | flops 5000000000 | bytes 30000000 | tf_op jit(solution)/shard_map/step/pallas_call | solution.py:323
  (13 shorter events, 0.0 us)
Async XLA Ops:
  1.3 26.8 %copy-start.1 = (s32[6,512]{1,0:T(8,128)S(1)}, s32[6,512]{1,0:T(8,128)}, u32[]{:S(2)}) copy-start(s32[6,512]{1,0:T(8,128)} %near_ref.7) | copy-start | bytes 36868
  1.3 26.8 %copy-start.4 = (f32[8]{0:T(128)S(1)}, f32[8]{0:T(128)}, u32[]{:S(2)}) copy-start(f32[8]{0:T(128)} %rates_ref.7) | copy-start | bytes 100
  3.7 7.0 %collective-permute-start = (f32[4,40,8,128]{3,2,1,0:T(8,128)S(1)}, f32[4,40,8,128]{3,2,1,0:T(8,128)S(1)}, u32[]{:S(2)}, u32[]{:S(2)}) collective-permute-start(f32[4,40,8,128]{3,2,1,0:T(8,128)S(1)} %get-tuple-element.25), channel_id=1, source_target_pairs={{0,1},{1,2},{2,3},{3,4},{4,5},{5,6},{6,7},{7,8},{8,9},{9,10},{10,1... | collective-permute-start | bytes 1966088 | tf_op jit(solution)/shard_map/ppermute | solution.py:308
  6.1 6.1 %collective-permute-start.1 = (f32[4,40,8,128]{3,2,1,0:T(8,128)S(1)}, f32[4,40,8,128]{3,2,1,0:T(8,128)S(1)}, u32[]{:S(2)}, u32[]{:S(2)}) collective-permute-start(f32[4,40,8,128]{3,2,1,0:T(8,128)S(1)} %get-tuple-element.22.refs_0_), channel_id=1, source_target_pairs={{1,0},{2,1},{3,2},{4,3},{5,4},{6,5},{7,6},{8,7},{9,8},{10,9},{11,1... | collective-permute-start | bytes 1966088 | tf_op jit(solution)/shard_map/ppermute | solution.py:308
  12.2 29.5 %collective-permute-start.2 = (f32[4,40,8,128]{3,2,1,0:T(8,128)}, f32[4,40,8,128]{3,2,1,0:T(8,128)S(1)}, u32[]{:S(2)}, u32[]{:S(2)}) collective-permute-start(f32[4,40,8,128]{3,2,1,0:T(8,128)} %get-tuple-element.26), channel_id=1, source_target_pairs={{0,1},{1,2},{2,3},{3,4},{4,5},{5,6},{6,7},{7,8},{8,9},{9,10},{10,1... | collective-permute-start | bytes 1966088 | tf_op jit(solution)/shard_map/ppermute | solution.py:308
  26.8 14.9 %collective-permute-start.3 = (f32[4,40,8,128]{3,2,1,0:T(8,128)}, f32[4,40,8,128]{3,2,1,0:T(8,128)}, u32[]{:S(2)}, u32[]{:S(2)}) collective-permute-start(f32[4,40,8,128]{3,2,1,0:T(8,128)} %get-tuple-element.27), channel_id=1, source_target_pairs={{1,0},{2,1},{3,2},{4,3},{5,4},{6,5},{7,6},{8,7},{9,8},{10,9},{11,1... | collective-permute-start | bytes 1966088 | tf_op jit(solution)/shard_map/ppermute | solution.py:308
  37.0 19.5 %collective-permute-start.6 = (f32[4,40,8,128]{3,2,1,0:T(8,128)}, f32[4,40,8,128]{3,2,1,0:T(8,128)S(1)}, u32[]{:S(2)}, u32[]{:S(2)}) collective-permute-start(f32[4,40,8,128]{3,2,1,0:T(8,128)} %get-tuple-element.34), channel_id=1, source_target_pairs={{0,1},{1,2},{2,3},{3,4},{4,5},{5,6},{6,7},{7,8},{8,9},{9,10},{10,1... | collective-permute-start | bytes 1966088 | tf_op jit(solution)/shard_map/ppermute | solution.py:308
  40.3 16.2 %collective-permute-start.7 = (f32[4,40,8,128]{3,2,1,0:T(8,128)S(1)}, f32[4,40,8,128]{3,2,1,0:T(8,128)}, u32[]{:S(2)}, u32[]{:S(2)}) collective-permute-start(f32[4,40,8,128]{3,2,1,0:T(8,128)S(1)} %get-tuple-element.30.refs_0_), channel_id=1, source_target_pairs={{1,0},{2,1},{3,2},{4,3},{5,4},{6,5},{7,6},{8,7},{9,8},{10,9},{11,1... | collective-permute-start | bytes 1966088 | tf_op jit(solution)/shard_map/ppermute | solution.py:308
  41.6 14.9 %copy-start.5 = (f32[4,8,8,8,512]{4,3,2,1,0:T(8,128)S(1)}, f32[4,8,8,8,512]{4,3,2,1,0:T(8,128)}, u32[]{:S(2)}) copy-start(f32[4,8,8,8,512]{4,3,2,1,0:T(8,128)} %get-tuple-element.35.u_ref) | copy-start | bytes 12582916
  50.8 35.0 %collective-permute-start.4 = (f32[4,40,8,128]{3,2,1,0:T(8,128)}, f32[4,40,8,128]{3,2,1,0:T(8,128)S(1)}, u32[]{:S(2)}, u32[]{:S(2)}) collective-permute-start(f32[4,40,8,128]{3,2,1,0:T(8,128)} %get-tuple-element.31), channel_id=1, source_target_pairs={{0,1},{1,2},{2,3},{3,4},{4,5},{5,6},{6,7},{7,8},{8,9},{9,10},{10,1... | collective-permute-start | bytes 1966088 | tf_op jit(solution)/shard_map/ppermute | solution.py:308
  55.0 30.7 %collective-permute-start.5 = (f32[4,40,8,128]{3,2,1,0:T(8,128)S(1)}, f32[4,40,8,128]{3,2,1,0:T(8,128)S(1)}, u32[]{:S(2)}, u32[]{:S(2)}) collective-permute-start(f32[4,40,8,128]{3,2,1,0:T(8,128)S(1)} %get-tuple-element.32.refs_0_), channel_id=1, source_target_pairs={{1,0},{2,1},{3,2},{4,3},{5,4},{6,5},{7,6},{8,7},{9,8},{10,9},{11,1... | collective-permute-start | bytes 1966088 | tf_op jit(solution)/shard_map/ppermute | solution.py:308
  56.5 8.1 %copy-start.2 = (f32[12,256]{1,0:T(8,128)S(1)}, f32[12,256]{1,0:T(8,128)}, u32[]{:S(2)}) copy-start(f32[12,256]{1,0:T(8,128)} %cond_ref.1) | copy-start | bytes 36868
  56.5 8.1 %copy-start.3 = (s32[512]{0:T(512)S(1)}, s32[512]{0:T(512)}, u32[]{:S(2)}) copy-start(s32[512]{0:T(512)} %param.9) | copy-start | bytes 6148
  79.7 6.1 %copy-start = (f32[4,8,8,8,512]{4,3,2,1,0:T(8,128)S(1)}, f32[4,8,8,8,512]{4,3,2,1,0:T(8,128)}, u32[]{:S(2)}) copy-start(f32[4,8,8,8,512]{4,3,2,1,0:T(8,128)} %get-tuple-element.33.u_ref) | copy-start | bytes 12582916

commit v5 on v4

--- a/solution.py
+++ b/solution.py
@@ -96,19 +96,21 @@
                 slots + (index & (EDGE - 1)),
                 jnp.where(index >= slots, index + EDGE, index),
             )
-            selector[face] = one_hot(index, slots + 2 * EDGE)
+            selector[face] = one_hot(index, selector.shape[1])
 
     own = [plane(u_ref, face) for face in range(6)]
     for face in range(6):
         rows = pair * size * size
-        table = jnp.concatenate(
-            [
-                own[face ^ 1].reshape(rows, slots),
-                read_edges(lower_ref, face ^ 1).reshape(rows, EDGE),
-                read_edges(upper_ref, face ^ 1).reshape(rows, EDGE),
-            ],
-            axis=1,
-        )
+        table = own[face ^ 1].reshape(rows, slots)
+        if lower_ref is not None:
+            table = jnp.concatenate(
+                [
+                    table,
+                    read_edges(lower_ref, face ^ 1).reshape(rows, EDGE),
+                    read_edges(upper_ref, face ^ 1).reshape(rows, EDGE),
+                ],
+                axis=1,
+            )
         taken = picked(table, selector[face]).reshape(pair, size, size, slots)
         outer = near_ref[face : face + 1, :] < 0
         ghosts[face] = jnp.where(outer, own[face], taken)
@@ -138,6 +140,59 @@
 def edge_step_kernel(start, base_ref, count_ref, rates_ref, near_ref, lower_ref, upper_ref, u_ref, *refs):
     out_ref, head_ref, tail_ref, selector, ghosts = refs[-5:]
     step_body(start, base_ref, count_ref, rates_ref, near_ref, lower_ref, upper_ref, u_ref, out_ref, selector, ghosts)
+    write_edges(out_ref, count_ref[0], head_ref, tail_ref)
+
+
+def local_step_kernel(start, base_ref, count_ref, rates_ref, near_ref, u_ref, out_ref, selector, ghosts):
+    step_body(start, base_ref, count_ref, rates_ref, near_ref, None, None, u_ref, out_ref, selector, ghosts)
+
+
+def remote_step_kernel(start, base_ref, count_ref, rates_ref, near_ref, lower_ref, upper_ref, u_ref,
+                       out_ref, head_ref, tail_ref, selector, ghosts):
+    pair, size, _, _, slots = u_ref.shape
+
+    @pl.when(pl.program_id(0) == 0)
+    def _():
+        for face in range(6):
+            index = near_ref[face : face + 1, :]
+            index = jnp.where(index < 0, FAR, index - base_ref[0])
+            beyond = jnp.where(index >= slots, index - slots + EDGE, -1)
+            index = jnp.where(index < 0, index & (EDGE - 1), beyond)
+            selector[face] = one_hot(index, 2 * EDGE)
+
+    for face in range(6):
+        rows = pair * size * size
+        table = jnp.concatenate(
+            [
+                read_edges(lower_ref, face ^ 1).reshape(rows, EDGE),
+                read_edges(upper_ref, face ^ 1).reshape(rows, EDGE),
+            ],
+            axis=1,
+        )
+        ghosts[face] = picked(table, selector[face]).reshape(pair, size, size, slots)
+
+    row = lax.broadcasted_iota(jnp.int32, (size, slots), 0)
+    first, last = row == 0, row == size - 1
+
+    def variable(v, carry):
+        live = lax.broadcasted_iota(jnp.int32, (1, slots), 1) < count_ref[0]
+        factor = jnp.where(live, rates_ref[start + pl.program_id(0) * pair + v], 0.0)
+        for i in range(size):
+            for j in range(size):
+                extra = jnp.where(first, ghosts[4, v, i, j : j + 1, :], 0.0)
+                extra = jnp.where(last, ghosts[5, v, i, j : j + 1, :], extra)
+                if i == 0:
+                    extra = extra + ghosts[0, v, j]
+                if i == size - 1:
+                    extra = extra + ghosts[1, v, j]
+                if j == 0:
+                    extra = extra + ghosts[2, v, i]
+                if j == size - 1:
+                    extra = extra + ghosts[3, v, i]
+                out_ref[v, i, j] = u_ref[v, i, j] + factor * extra
+        return carry
+
+    lax.fori_loop(0, pair, variable, 0)
     write_edges(out_ref, count_ref[0], head_ref, tail_ref)
 
 
@@ -319,16 +374,18 @@
             name="edges",
         )(counts, state, *after)
 
-    def step(kernel, start, u, halo, out_specs, out_shape, extra=(), extra_specs=(), aliases={}):
+    def step(kernel, start, u, halo, out_specs, out_shape, extra=(), extra_specs=(), aliases={}, depth=slots + 2 * EDGE):
         return pl.pallas_call(
             functools.partial(kernel, start),
             grid=grid,
-            in_specs=[smem(), smem(), smem(), near, edge, edge, block(start if u is state else 0)]
+            in_specs=[smem(), smem(), smem(), near]
+            + [edge] * len(halo)
+            + [block(start if u is state else 0)]
             + list(extra_specs),
             out_specs=out_specs,
             out_shape=out_shape,
             scratch_shapes=[
-                pltpu.VMEM((6, slots + 2 * EDGE, slots), BF16),
+                pltpu.VMEM((6, depth, slots), BF16),
                 pltpu.VMEM((6, PAIR, size, size, slots), F32),
             ],
             input_output_aliases=aliases,
@@ -339,12 +396,13 @@
 
     head_b, tail_b = edges(half)
     halo_b = exchange(head_b, tail_b)
-    head_a, tail_a = edges(0, head_b)
+    u_b = step(local_step_kernel, half, state, (), block(0), part, depth=slots)
+    head_a, tail_a = edges(0, u_b)
     head_a, tail_a, *halo_b = lax.optimization_barrier((head_a, tail_a, *halo_b))
     halo_a = exchange(head_a, tail_a)
     outs = [block(0), edge, edge]
     shapes = [part, edge_shape, edge_shape]
-    u_b, head_b, tail_b = step(edge_step_kernel, half, state, halo_b, outs, shapes)
+    u_b, head_b, tail_b = step(remote_step_kernel, half, u_b, halo_b, outs, shapes, depth=2 * EDGE)
     halo_b = exchange(head_b, tail_b)
     u_a, head_a, tail_a = step(edge_step_kernel, 0, state, halo_a, outs, shapes, (head_b,), (anywhere,))
     halo_a = exchange(head_a, tail_a)

time: 94.3 us -> 99.6 us (1.056)
  Pallas kernels: 60.9 us -> 70.2 us
  starting transfers between devices: 30 us -> 27.5 us
  waiting for transfers between devices: 1.5 us -> 0.02 us
    pallas_call x4 -> x5, Pallas kernels: 34.2 us -> 39.5 us  [step(): pl.pallas_call(functools.partial(kernel, start), grid=grid, in_specs=[sme...]
    pallas_call x1, Pallas kernels: 15 us -> 17.6 us  [on_device(): pl.pallas_call(functools.partial(spread_kernel, groups, blks), in_specs=[...]
    ppermute x8, starting transfers between devices: 30 us -> 27.5 us  [exchange(): return (lax.ppermute(tail, axes, up), lax.ppermute(head, axes, down))]
    ppermute x8, waiting for transfers between devices: 1.5 us -> 0.02 us  [exchange(): return (lax.ppermute(tail, axes, up), lax.ppermute(head, axes, down))]
    pallas_call x2, Pallas kernels: 5.65 us -> 7.02 us  [edges(): pl.pallas_call(edges_kernel, grid=grid, in_specs=[smem(), block(start)] +...]
  transfers between devices with their start and end apart: 8 -> 8, of which waited for: 1 -> 0; matrix products, arithmetic and copies ran while one was open for 0% -> 0% of each run, Pallas kernels for 54% -> 60%
where the time goes in v5:
time: 99.6 us; the launch traced here: 99.3 us
  Pallas kernels  70.2 us (70%)
  starting transfers between devices  27.5 us (28%)
  between operations  1.52 us (2%)
    pallas_call x5, Pallas kernels, step(): pl.pallas_call(functools.partial(kernel, start), grid=grid, in_specs=[sme...  39.5 us
    ppermute x8, starting transfers between devices, exchange(): return (lax.ppermute(tail, axes, up), lax.ppermute(head, axes, down))  27.5 us
    pallas_call x1, Pallas kernels, on_device(): pl.pallas_call(functools.partial(spread_kernel, groups, blks), in_specs=[...  17.6 us
    pallas_call x2, Pallas kernels, edges(): pl.pallas_call(edges_kernel, grid=grid, in_specs=[smem(), block(start)] +...  7.02 us
    pallas_call x1, Pallas kernels, on_device(): pl.pallas_call(functools.partial(grid_kernel, lons.bit_length() - 1), gri...  6.06 us
  transfers between devices with their start and end apart: 8, of which 0 were waited for; matrix products, arithmetic and copies ran while one was open for 0% of the time, Pallas kernels for 60%

profile of v5, /device:TPU:0, one launch (start us, length us, event | category | flops | bytes accessed | tf_op | source)
XLA Modules:
  0.0 99.3 jit_solution(11918759708792458973)
XLA Ops:
  1.3 2.4 %edges.3 = (f32[4,40,8,128]{3,2,1,0:T(8,128)S(1)}, f32[4,40,8,128]{3,2,1,0:T(8,128)S(1)}) custom-call(s32[1]{0:T(128)S(6)} %copy.10.count_ref, f32[8,8,8,8,512]{4,3,2,1,0:T(8,128)} %u_ref.7), custom_call_target="tpu_custom_call" | custom-call | flops 1000000 | bytes 8000000 | tf_op jit(solution)/shard_map/edges/pallas_call | solution.py:366
  3.7 2.4 %collective-permute-start = (f32[4,40,8,128]{3,2,1,0:T(8,128)S(1)}, f32[4,40,8,128]{3,2,1,0:T(8,128)S(1)}, u32[]{:S(2)}, u32[]{:S(2)}) collective-permute-start(f32[4,40,8,128]{3,2,1,0:T(8,128)S(1)} %get-tuple-element.24), channel_id=1, source_target_pairs={{0,1},{1,2},{2,3},{3,4},{4,5},{5,6},{6,7},{7,8},{8,9},{9,10},{10,1... | collective-permute-start | bytes 1966088 | tf_op jit(solution)/shard_map/ppermute | solution.py:363
  6.1 1.3 %collective-permute-start.1 = (f32[4,40,8,128]{3,2,1,0:T(8,128)S(1)}, f32[4,40,8,128]{3,2,1,0:T(8,128)S(1)}, u32[]{:S(2)}, u32[]{:S(2)}) collective-permute-start(f32[4,40,8,128]{3,2,1,0:T(8,128)S(1)} %get-tuple-element.25), channel_id=1, source_target_pairs={{1,0},{2,1},{3,2},{4,3},{5,4},{6,5},{7,6},{8,7},{9,8},{10,9},{11,1... | collective-permute-start | bytes 1966088 | tf_op jit(solution)/shard_map/ppermute | solution.py:363
  7.4 8.7 %step.5.refs_0_.u_ref = f32[4,8,8,8,512]{4,3,2,1,0:T(8,128)S(1)} custom-call(s32[1]{0:T(128)} %bitcast.base_ref, s32[1]{0:T(128)S(6)} %copy.10.count_ref, f32[8]{0:T(128)S(1)} %copy-done.5, s32[6,512]{1,0:T(8,128)S(1)} %copy-done.2, f32[8,8,8,8,512]{4,3,2,1,0:T(8,128)} %u_ref.7), custom_call_target="tpu_custom_call" | custom-call | flops 5000000000 | bytes 30000000 | tf_op jit(solution)/shard_map/step/pallas_call | solution.py:378
  16.2 0.0 copy-start
  16.2 4.6 %edges.2 = (f32[4,40,8,128]{3,2,1,0:T(8,128)S(1)}, f32[4,40,8,128]{3,2,1,0:T(8,128)}) custom-call(s32[1]{0:T(128)S(6)} %copy.10.count_ref, f32[8,8,8,8,512]{4,3,2,1,0:T(8,128)} %u_ref.7, f32[4,8,8,8,512]{4,3,2,1,0:T(8,128)S(1)} %step.5.refs_0_.u_ref), custom_call_target="tpu_custom_call" | custom-call | flops 1000000 | bytes 8000000 | tf_op jit(solution)/shard_map/edges/pallas_call | solution.py:366
  20.8 0.0 collective-permute-done.lower_ref
  20.8 0.0 collective-permute-done.1.upper_ref
  20.8 6.8 %collective-permute-start.2 = (f32[4,40,8,128]{3,2,1,0:T(8,128)}, f32[4,40,8,128]{3,2,1,0:T(8,128)}, u32[]{:S(2)}, u32[]{:S(2)}) collective-permute-start(f32[4,40,8,128]{3,2,1,0:T(8,128)} %get-tuple-element.26), channel_id=1, source_target_pairs={{0,1},{1,2},{2,3},{3,4},{4,5},{5,6},{6,7},{7,8},{8,9},{9,10},{10,1... | collective-permute-start | bytes 1966088 | tf_op jit(solution)/shard_map/ppermute | solution.py:363
  27.7 1.3 %collective-permute-start.3 = (f32[4,40,8,128]{3,2,1,0:T(8,128)S(1)}, f32[4,40,8,128]{3,2,1,0:T(8,128)}, u32[]{:S(2)}, u32[]{:S(2)}) collective-permute-start(f32[4,40,8,128]{3,2,1,0:T(8,128)S(1)} %get-tuple-element.27), channel_id=1, source_target_pairs={{1,0},{2,1},{3,2},{4,3},{5,4},{6,5},{7,6},{8,7},{9,8},{10,9},{11,1... | collective-permute-start | bytes 1966088 | tf_op jit(solution)/shard_map/ppermute | solution.py:363
  29.0 5.4 %step.6 = (f32[4,8,8,8,512]{4,3,2,1,0:T(8,128)}, f32[4,40,8,128]{3,2,1,0:T(8,128)S(1)}, f32[4,40,8,128]{3,2,1,0:T(8,128)}) custom-call(s32[1]{0:T(128)} %bitcast.base_ref, s32[1]{0:T(128)S(6)} %copy.10.count_ref, f32[8]{0:T(128)S(1)} %copy-done.5, s32[6,512]{1,0:T(8,128)S(1)} %copy-done.2, f32[4,40,8,128]{3,2,1,0:T(8,128)S(1)} %collective-permute-done.lower_ref, ...), custom_call_target="tpu_custom_call" | custom-call | flops 5000000000 | bytes 30000000 | tf_op jit(solution)/shard_map/step/pallas_call | solution.py:378
  34.3 3.1 %collective-permute-start.6 = (f32[4,40,8,128]{3,2,1,0:T(8,128)}, f32[4,40,8,128]{3,2,1,0:T(8,128)S(1)}, u32[]{:S(2)}, u32[]{:S(2)}) collective-permute-start(f32[4,40,8,128]{3,2,1,0:T(8,128)} %get-tuple-element.34), channel_id=1, source_target_pairs={{0,1},{1,2},{2,3},{3,4},{4,5},{5,6},{6,7},{7,8},{8,9},{9,10},{10,1... | collective-permute-start | bytes 1966088 | tf_op jit(solution)/shard_map/ppermute | solution.py:363
  37.4 1.3 %collective-permute-start.7 = (f32[4,40,8,128]{3,2,1,0:T(8,128)S(1)}, f32[4,40,8,128]{3,2,1,0:T(8,128)}, u32[]{:S(2)}, u32[]{:S(2)}) collective-permute-start(f32[4,40,8,128]{3,2,1,0:T(8,128)S(1)} %get-tuple-element.30.refs_0_), channel_id=1, source_target_pairs={{1,0},{2,1},{3,2},{4,3},{5,4},{6,5},{7,6},{8,7},{9,8},{10,9},{11,1... | collective-permute-start | bytes 1966088 | tf_op jit(solution)/shard_map/ppermute | solution.py:363
  38.7 0.0 collective-permute-done.2.lower_ref
  38.7 9.2 %step.7 = (f32[4,8,8,8,512]{4,3,2,1,0:T(8,128)}, f32[4,40,8,128]{3,2,1,0:T(8,128)S(1)}, f32[4,40,8,128]{3,2,1,0:T(8,128)}) custom-call(s32[1]{0:T(128)} %bitcast.base_ref, s32[1]{0:T(128)S(6)} %copy.10.count_ref, f32[8]{0:T(128)S(1)} %copy-done.5, s32[6,512]{1,0:T(8,128)S(1)} %copy-done.2, f32[4,40,8,128]{3,2,1,0:T(8,128)} %collective-permute-done.2.lower_ref, ...), custom_call_target="tpu_custom_call" | custom-call | flops 5000000000 | bytes 30000000 | tf_op jit(solution)/shard_map/step/pallas_call | solution.py:378
  47.9 9.8 %collective-permute-start.4 = (f32[4,40,8,128]{3,2,1,0:T(8,128)}, f32[4,40,8,128]{3,2,1,0:T(8,128)S(1)}, u32[]{:S(2)}, u32[]{:S(2)}) collective-permute-start(f32[4,40,8,128]{3,2,1,0:T(8,128)} %get-tuple-element.31), channel_id=1, source_target_pairs={{0,1},{1,2},{2,3},{3,4},{4,5},{5,6},{6,7},{7,8},{8,9},{9,10},{10,1... | collective-permute-start | bytes 1966088 | tf_op jit(solution)/shard_map/ppermute | solution.py:363
  57.8 1.5 %collective-permute-start.5 = (f32[4,40,8,128]{3,2,1,0:T(8,128)S(1)}, f32[4,40,8,128]{3,2,1,0:T(8,128)S(1)}, u32[]{:S(2)}, u32[]{:S(2)}) collective-permute-start(f32[4,40,8,128]{3,2,1,0:T(8,128)S(1)} %get-tuple-element.32.refs_0_), channel_id=1, source_target_pairs={{1,0},{2,1},{3,2},{4,3},{5,4},{6,5},{7,6},{8,7},{9,8},{10,9},{11,1... | collective-permute-start | bytes 1966088 | tf_op jit(solution)/shard_map/ppermute | solution.py:363
  59.3 0.0 collective-permute-done.6.lower_ref
  59.3 0.0 copy-start.3
  59.3 0.0 copy-start.4
  59.3 8.0 %step.8 = (f32[8,8,8,8,512]{4,3,2,1,0:T(8,128)}, f32[2,2,512]{2,1,0:T(2,128)S(1)}) custom-call(s32[1]{0:T(128)} %bitcast.base_ref, s32[1]{0:T(128)S(6)} %copy.10.count_ref, f32[8]{0:T(128)S(1)} %copy-done.5, s32[6,512]{1,0:T(8,128)S(1)} %copy-done.2, f32[4,40,8,128]{3,2,1,0:T(8,128)S(1)} %collective-permute-done.6.lower_ref, ...), custom_call_target="tpu_custom_call" | custom-call | flops 5000000000 | bytes 30000000 | tf_op jit(solution)/shard_map/step/pallas_call | solution.py:378
  67.4 17.6 %spread.1 = (f32[32,2,512]{2,1,0:T(2,128)S(1)}, f32[96,256]{1,0:T(8,128)S(1)}) custom-call(s32[1,512]{1,0:T(1,128)S(1)} %bitcast.3, f32[4,512]{1,0:T(4,128)S(1)} %reshape.19.faces_ref, f32[12,256]{1,0:T(8,128)S(1)} %copy-done.3), custom_call_target="tpu_custom_call" | custom-call | tf_op jit(solution)/shard_map/spread/pallas_call | solution.py:415
  85.0 6.1 %ionosphere.1 = (f32[1,512]{1,0:T(1,128)S(1)}, f32[12,256]{1,0:T(8,128)}) custom-call(s32[1]{0:T(128)} %bitcast.1.first_ref, f32[32,2,512]{2,1,0:T(2,128)S(1)} %get-tuple-element.37.parts_ref, f32[96,256]{1,0:T(8,128)S(1)} %get-tuple-element.38.cond_ref, s32[1,512]{1,0:T(1,128)S(1)} %bitcast.4), custom_call_target="tpu_custom_call" | custom-call | flops 5000000000 | bytes 1000000 | tf_op jit(solution)/shard_map/ionosphere/pallas_call | solution.py:439
  91.1 8.2 %step.9 = f32[8,8,8,8,512]{4,3,2,1,0:T(8,128)} custom-call(s32[1]{0:T(128)} %bitcast.base_ref, s32[1]{0:T(128)S(6)} %copy.10.count_ref, f32[8]{0:T(128)S(1)} %copy-done.5, s32[6,512]{1,0:T(8,128)S(1)} %copy-done.2, f32[4,40,8,128]{3,2,1,0:T(8,128)S(1)} %collective-permute-done.4.lower_ref, ...), custom_call_target="tpu_custom_call", output_to_operand_aliasing={{}: (8, {})} | custom-call | flops 5000000000 | bytes 30000000 | tf_op jit(solution)/shard_map/step/pallas_call | solution.py:378
  (16 shorter events, 0.0 us)
Async XLA Ops:
  0.6 6.8 %copy-start.5 = (f32[8]{0:T(128)S(1)}, f32[8]{0:T(128)}, u32[]{:S(2)}) copy-start(f32[8]{0:T(128)} %rates_ref.9) | copy-start | bytes 100
  0.6 6.8 %copy-start.2 = (s32[6,512]{1,0:T(8,128)S(1)}, s32[6,512]{1,0:T(8,128)}, u32[]{:S(2)}) copy-start(s32[6,512]{1,0:T(8,128)} %near_ref.9) | copy-start | bytes 36868
  3.7 17.1 %collective-permute-start = (f32[4,40,8,128]{3,2,1,0:T(8,128)S(1)}, f32[4,40,8,128]{3,2,1,0:T(8,128)S(1)}, u32[]{:S(2)}, u32[]{:S(2)}) collective-permute-start(f32[4,40,8,128]{3,2,1,0:T(8,128)S(1)} %get-tuple-element.24), channel_id=1, source_target_pairs={{0,1},{1,2},{2,3},{3,4},{4,5},{5,6},{6,7},{7,8},{8,9},{9,10},{10,1... | collective-permute-start | bytes 1966088 | tf_op jit(solution)/shard_map/ppermute | solution.py:363
  6.1 14.7 %collective-permute-start.1 = (f32[4,40,8,128]{3,2,1,0:T(8,128)S(1)}, f32[4,40,8,128]{3,2,1,0:T(8,128)S(1)}, u32[]{:S(2)}, u32[]{:S(2)}) collective-permute-start(f32[4,40,8,128]{3,2,1,0:T(8,128)S(1)} %get-tuple-element.25), channel_id=1, source_target_pairs={{1,0},{2,1},{3,2},{4,3},{5,4},{6,5},{7,6},{8,7},{9,8},{10,9},{11,1... | collective-permute-start | bytes 1966088 | tf_op jit(solution)/shard_map/ppermute | solution.py:363
  16.2 12.8 %copy-start = (f32[4,8,8,8,512]{4,3,2,1,0:T(8,128)}, f32[4,8,8,8,512]{4,3,2,1,0:T(8,128)S(1)}, u32[]{:S(2)}) copy-start(f32[4,8,8,8,512]{4,3,2,1,0:T(8,128)S(1)} %step.5.refs_0_.u_ref) | copy-start | bytes 12582916
  20.8 17.9 %collective-permute-start.2 = (f32[4,40,8,128]{3,2,1,0:T(8,128)}, f32[4,40,8,128]{3,2,1,0:T(8,128)}, u32[]{:S(2)}, u32[]{:S(2)}) collective-permute-start(f32[4,40,8,128]{3,2,1,0:T(8,128)} %get-tuple-element.26), channel_id=1, source_target_pairs={{0,1},{1,2},{2,3},{3,4},{4,5},{5,6},{6,7},{7,8},{8,9},{9,10},{10,1... | collective-permute-start | bytes 1966088 | tf_op jit(solution)/shard_map/ppermute | solution.py:363
  27.7 11.1 %collective-permute-start.3 = (f32[4,40,8,128]{3,2,1,0:T(8,128)S(1)}, f32[4,40,8,128]{3,2,1,0:T(8,128)}, u32[]{:S(2)}, u32[]{:S(2)}) collective-permute-start(f32[4,40,8,128]{3,2,1,0:T(8,128)S(1)} %get-tuple-element.27), channel_id=1, source_target_pairs={{1,0},{2,1},{3,2},{4,3},{5,4},{6,5},{7,6},{8,7},{9,8},{10,9},{11,1... | collective-permute-start | bytes 1966088 | tf_op jit(solution)/shard_map/ppermute | solution.py:363
  34.3 24.9 %collective-permute-start.6 = (f32[4,40,8,128]{3,2,1,0:T(8,128)}, f32[4,40,8,128]{3,2,1,0:T(8,128)S(1)}, u32[]{:S(2)}, u32[]{:S(2)}) collective-permute-start(f32[4,40,8,128]{3,2,1,0:T(8,128)} %get-tuple-element.34), channel_id=1, source_target_pairs={{0,1},{1,2},{2,3},{3,4},{4,5},{5,6},{6,7},{7,8},{8,9},{9,10},{10,1... | collective-permute-start | bytes 1966088 | tf_op jit(solution)/shard_map/ppermute | solution.py:363
  37.4 21.8 %collective-permute-start.7 = (f32[4,40,8,128]{3,2,1,0:T(8,128)S(1)}, f32[4,40,8,128]{3,2,1,0:T(8,128)}, u32[]{:S(2)}, u32[]{:S(2)}) collective-permute-start(f32[4,40,8,128]{3,2,1,0:T(8,128)S(1)} %get-tuple-element.30.refs_0_), channel_id=1, source_target_pairs={{1,0},{2,1},{3,2},{4,3},{5,4},{6,5},{7,6},{8,7},{9,8},{10,9},{11,1... | collective-permute-start | bytes 1966088 | tf_op jit(solution)/shard_map/ppermute | solution.py:363
  38.7 20.6 %copy-start.6 = (f32[4,8,8,8,512]{4,3,2,1,0:T(8,128)S(1)}, f32[4,8,8,8,512]{4,3,2,1,0:T(8,128)}, u32[]{:S(2)}) copy-start(f32[4,8,8,8,512]{4,3,2,1,0:T(8,128)} %get-tuple-element.35.u_ref) | copy-start | bytes 12582916
  47.9 43.1 %collective-permute-start.4 = (f32[4,40,8,128]{3,2,1,0:T(8,128)}, f32[4,40,8,128]{3,2,1,0:T(8,128)S(1)}, u32[]{:S(2)}, u32[]{:S(2)}) collective-permute-start(f32[4,40,8,128]{3,2,1,0:T(8,128)} %get-tuple-element.31), channel_id=1, source_target_pairs={{0,1},{1,2},{2,3},{3,4},{4,5},{5,6},{6,7},{7,8},{8,9},{9,10},{10,1... | collective-permute-start | bytes 1966088 | tf_op jit(solution)/shard_map/ppermute | solution.py:363
  57.8 33.3 %collective-permute-start.5 = (f32[4,40,8,128]{3,2,1,0:T(8,128)S(1)}, f32[4,40,8,128]{3,2,1,0:T(8,128)S(1)}, u32[]{:S(2)}, u32[]{:S(2)}) collective-permute-start(f32[4,40,8,128]{3,2,1,0:T(8,128)S(1)} %get-tuple-element.32.refs_0_), channel_id=1, source_target_pairs={{1,0},{2,1},{3,2},{4,3},{5,4},{6,5},{7,6},{8,7},{9,8},{10,9},{11,1... | collective-permute-start | bytes 1966088 | tf_op jit(solution)/shard_map/ppermute | solution.py:363
  59.3 8.1 %copy-start.3 = (f32[12,256]{1,0:T(8,128)S(1)}, f32[12,256]{1,0:T(8,128)}, u32[]{:S(2)}) copy-start(f32[12,256]{1,0:T(8,128)} %cond_ref.1) | copy-start | bytes 36868
  59.3 8.1 %copy-start.4 = (s32[512]{0:T(512)S(1)}, s32[512]{0:T(512)}, u32[]{:S(2)}) copy-start(s32[512]{0:T(512)} %param.9) | copy-start | bytes 6148
  85.0 6.1 %copy-start.1 = (f32[4,8,8,8,512]{4,3,2,1,0:T(8,128)S(1)}, f32[4,8,8,8,512]{4,3,2,1,0:T(8,128)}, u32[]{:S(2)}) copy-start(f32[4,8,8,8,512]{4,3,2,1,0:T(8,128)} %get-tuple-element.33.u_ref) | copy-start | bytes 12582916

commit v6 on v4

--- a/solution.py
+++ b/solution.py
@@ -10,7 +10,7 @@
 ITERS = 3
 EDGE = 128
 FAR = 1 << 29
-PAIR = 2
+PAIR = 4
 VMEM_LIMIT = 48 * 1024 * 1024
 BF16 = jnp.bfloat16
 F32 = jnp.float32

time: 94.3 us -> 93.5 us (level)
  no operation moved by 1% of the time
where the time goes in v6:
time: 93.5 us; the launch traced here: 93.1 us
  Pallas kernels  60.2 us (64%)
  starting transfers between devices  30 us (32%)
  between operations  1.46 us (2%)
  waiting for transfers between devices  1.41 us (2%)
    pallas_call x4, Pallas kernels, step(): pl.pallas_call(functools.partial(kernel, start), grid=grid, in_specs=[sme...  33.3 us
    ppermute x8, starting transfers between devices, exchange(): return (lax.ppermute(tail, axes, up), lax.ppermute(head, axes, down))  30 us
    pallas_call x1, Pallas kernels, on_device(): pl.pallas_call(functools.partial(spread_kernel, groups, blks), in_specs=[...  14.9 us
    pallas_call x1, Pallas kernels, on_device(): pl.pallas_call(functools.partial(grid_kernel, lons.bit_length() - 1), gri...  6.06 us
    pallas_call x2, Pallas kernels, edges(): pl.pallas_call(edges_kernel, grid=grid, in_specs=[smem(), block(start)] +...  5.87 us
  transfers between devices with their start and end apart: 8, of which 1 were waited for; matrix products, arithmetic and copies ran while one was open for 0% of the time, Pallas kernels for 54%

profile of v6, /device:TPU:0, one launch (start us, length us, event | category | flops | bytes accessed | tf_op | source)
XLA Modules:
  0.0 93.1 jit_solution(13293892561813653678)
XLA Ops:
  1.3 2.5 %edges.2 = (f32[4,40,8,128]{3,2,1,0:T(8,128)S(1)}, f32[4,40,8,128]{3,2,1,0:T(8,128)S(1)}) custom-call(s32[1]{0:T(128)S(6)} %copy.10.count_ref, f32[8,8,8,8,512]{4,3,2,1,0:T(8,128)} %u_ref.7), custom_call_target="tpu_custom_call" | custom-call | flops 1000000 | bytes 8000000 | tf_op jit(solution)/shard_map/edges/pallas_call | solution.py:311
  3.8 2.4 %collective-permute-start = (f32[4,40,8,128]{3,2,1,0:T(8,128)S(1)}, f32[4,40,8,128]{3,2,1,0:T(8,128)S(1)}, u32[]{:S(2)}, u32[]{:S(2)}) collective-permute-start(f32[4,40,8,128]{3,2,1,0:T(8,128)S(1)} %get-tuple-element.25), channel_id=1, source_target_pairs={{0,1},{1,2},{2,3},{3,4},{4,5},{5,6},{6,7},{7,8},{8,9},{9,10},{10,1... | collective-permute-start | bytes 1966088 | tf_op jit(solution)/shard_map/ppermute | solution.py:308
  6.2 1.3 %collective-permute-start.1 = (f32[4,40,8,128]{3,2,1,0:T(8,128)S(1)}, f32[4,40,8,128]{3,2,1,0:T(8,128)S(1)}, u32[]{:S(2)}, u32[]{:S(2)}) collective-permute-start(f32[4,40,8,128]{3,2,1,0:T(8,128)S(1)} %get-tuple-element.22.refs_0_), channel_id=1, source_target_pairs={{1,0},{2,1},{3,2},{4,3},{5,4},{6,5},{7,6},{8,7},{9,8},{10,9},{11,1... | collective-permute-start | bytes 1966088 | tf_op jit(solution)/shard_map/ppermute | solution.py:308
  7.5 3.4 %edges.3 = (f32[4,40,8,128]{3,2,1,0:T(8,128)S(1)}, f32[4,40,8,128]{3,2,1,0:T(8,128)}) custom-call(s32[1]{0:T(128)S(6)} %copy.10.count_ref, f32[8,8,8,8,512]{4,3,2,1,0:T(8,128)} %u_ref.7, f32[4,40,8,128]{3,2,1,0:T(8,128)S(1)} %get-tuple-element.22.refs_0_), custom_call_target="tpu_custom_call" | custom-call | flops 1000000 | bytes 8000000 | tf_op jit(solution)/shard_map/edges/pallas_call | solution.py:311
  10.9 0.0 collective-permute-done.lower_ref
  10.9 1.4 %collective-permute-done.1.upper_ref = f32[4,40,8,128]{3,2,1,0:T(8,128)S(1)} collective-permute-done((f32[4,40,8,128]{3,2,1,0:T(8,128)S(1)}, f32[4,40,8,128]{3,2,1,0:T(8,128)S(1)}, u32[]{:S(2)}, u32[]{:S(2)}) %collective-permute-start.1) | collective-permute-done | bytes 655392 | tf_op jit(solution)/shard_map/ppermute | solution.py:308
  12.3 15.4 %collective-permute-start.2 = (f32[4,40,8,128]{3,2,1,0:T(8,128)}, f32[4,40,8,128]{3,2,1,0:T(8,128)}, u32[]{:S(2)}, u32[]{:S(2)}) collective-permute-start(f32[4,40,8,128]{3,2,1,0:T(8,128)} %get-tuple-element.26), channel_id=1, source_target_pairs={{0,1},{1,2},{2,3},{3,4},{4,5},{5,6},{6,7},{7,8},{8,9},{9,10},{10,1... | collective-permute-start | bytes 1966088 | tf_op jit(solution)/shard_map/ppermute | solution.py:308
  27.7 1.3 %collective-permute-start.3 = (f32[4,40,8,128]{3,2,1,0:T(8,128)S(1)}, f32[4,40,8,128]{3,2,1,0:T(8,128)}, u32[]{:S(2)}, u32[]{:S(2)}) collective-permute-start(f32[4,40,8,128]{3,2,1,0:T(8,128)S(1)} %get-tuple-element.27), channel_id=1, source_target_pairs={{1,0},{2,1},{3,2},{4,3},{5,4},{6,5},{7,6},{8,7},{9,8},{10,9},{11,1... | collective-permute-start | bytes 1966088 | tf_op jit(solution)/shard_map/ppermute | solution.py:308
  29.0 9.0 %step.4 = (f32[4,8,8,8,512]{4,3,2,1,0:T(8,128)}, f32[4,40,8,128]{3,2,1,0:T(8,128)S(1)}, f32[4,40,8,128]{3,2,1,0:T(8,128)}) custom-call(s32[1]{0:T(128)} %bitcast.base_ref, s32[1]{0:T(128)S(6)} %copy.10.count_ref, f32[8]{0:T(128)S(1)} %copy-done.4, s32[6,512]{1,0:T(8,128)S(1)} %copy-done.1, f32[4,40,8,128]{3,2,1,0:T(8,128)S(1)} %collective-permute-done.lower_ref, ...), custom_call_target="tpu_custom_call" | custom-call | flops 5000000000 | bytes 30000000 | tf_op jit(solution)/shard_map/step/pallas_call | solution.py:323
  38.1 3.1 %collective-permute-start.6 = (f32[4,40,8,128]{3,2,1,0:T(8,128)}, f32[4,40,8,128]{3,2,1,0:T(8,128)S(1)}, u32[]{:S(2)}, u32[]{:S(2)}) collective-permute-start(f32[4,40,8,128]{3,2,1,0:T(8,128)} %get-tuple-element.34), channel_id=1, source_target_pairs={{0,1},{1,2},{2,3},{3,4},{4,5},{5,6},{6,7},{7,8},{8,9},{9,10},{10,1... | collective-permute-start | bytes 1966088 | tf_op jit(solution)/shard_map/ppermute | solution.py:308
  41.1 1.3 %collective-permute-start.7 = (f32[4,40,8,128]{3,2,1,0:T(8,128)S(1)}, f32[4,40,8,128]{3,2,1,0:T(8,128)S(1)}, u32[]{:S(2)}, u32[]{:S(2)}) collective-permute-start(f32[4,40,8,128]{3,2,1,0:T(8,128)S(1)} %get-tuple-element.30.refs_0_), channel_id=1, source_target_pairs={{1,0},{2,1},{3,2},{4,3},{5,4},{6,5},{7,6},{8,7},{9,8},{10,9},{11,1... | collective-permute-start | bytes 1966088 | tf_op jit(solution)/shard_map/ppermute | solution.py:308
  42.4 0.0 copy-start.5
  42.4 0.0 collective-permute-done.2.lower_ref
  42.5 9.3 %step.5 = (f32[4,8,8,8,512]{4,3,2,1,0:T(8,128)}, f32[4,40,8,128]{3,2,1,0:T(8,128)S(1)}, f32[4,40,8,128]{3,2,1,0:T(8,128)S(1)}) custom-call(s32[1]{0:T(128)} %bitcast.base_ref, s32[1]{0:T(128)S(6)} %copy.10.count_ref, f32[8]{0:T(128)S(1)} %copy-done.4, s32[6,512]{1,0:T(8,128)S(1)} %copy-done.1, f32[4,40,8,128]{3,2,1,0:T(8,128)} %collective-permute-done.2.lower_ref, ...), custom_call_target="tpu_custom_call" | custom-call | flops 5000000000 | bytes 30000000 | tf_op jit(solution)/shard_map/step/pallas_call | solution.py:323
  51.8 3.8 %collective-permute-start.4 = (f32[4,40,8,128]{3,2,1,0:T(8,128)S(1)}, f32[4,40,8,128]{3,2,1,0:T(8,128)S(1)}, u32[]{:S(2)}, u32[]{:S(2)}) collective-permute-start(f32[4,40,8,128]{3,2,1,0:T(8,128)S(1)} %get-tuple-element.31), channel_id=1, source_target_pairs={{0,1},{1,2},{2,3},{3,4},{4,5},{5,6},{6,7},{7,8},{8,9},{9,10},{10,1... | collective-permute-start | bytes 1966088 | tf_op jit(solution)/shard_map/ppermute | solution.py:308
  55.6 1.5 %collective-permute-start.5 = (f32[4,40,8,128]{3,2,1,0:T(8,128)S(1)}, f32[4,40,8,128]{3,2,1,0:T(8,128)S(1)}, u32[]{:S(2)}, u32[]{:S(2)}) collective-permute-start(f32[4,40,8,128]{3,2,1,0:T(8,128)S(1)} %get-tuple-element.32.refs_0_), channel_id=1, source_target_pairs={{1,0},{2,1},{3,2},{4,3},{5,4},{6,5},{7,6},{8,7},{9,8},{10,9},{11,1... | collective-permute-start | bytes 1966088 | tf_op jit(solution)/shard_map/ppermute | solution.py:308
  57.0 0.0 collective-permute-done.6.lower_ref
  57.1 0.0 copy-start.2
  57.1 0.0 copy-start.3
  57.1 7.2 %step.6 = (f32[8,8,8,8,512]{4,3,2,1,0:T(8,128)}, f32[1,4,512]{2,1,0:T(4,128)S(1)}) custom-call(s32[1]{0:T(128)} %bitcast.base_ref, s32[1]{0:T(128)S(6)} %copy.10.count_ref, f32[8]{0:T(128)S(1)} %copy-done.4, s32[6,512]{1,0:T(8,128)S(1)} %copy-done.1, f32[4,40,8,128]{3,2,1,0:T(8,128)S(1)} %collective-permute-done.6.lower_ref, ...), custom_call_target="tpu_custom_call" | custom-call | flops 5000000000 | bytes 30000000 | tf_op jit(solution)/shard_map/step/pallas_call | solution.py:323
  64.3 14.9 %spread.1 = (f32[32,2,512]{2,1,0:T(2,128)S(1)}, f32[96,256]{1,0:T(8,128)S(1)}) custom-call(s32[1,512]{1,0:T(1,128)S(1)} %bitcast.5, f32[4,512]{1,0:T(4,128)S(1)} %bitcast.4, f32[12,256]{1,0:T(8,128)S(1)} %copy-done.2), custom_call_target="tpu_custom_call" | custom-call | tf_op jit(solution)/shard_map/spread/pallas_call | solution.py:357
  79.3 6.1 %ionosphere.1 = (f32[1,512]{1,0:T(1,128)S(1)}, f32[12,256]{1,0:T(8,128)}) custom-call(s32[1]{0:T(128)} %bitcast.1.first_ref, f32[32,2,512]{2,1,0:T(2,128)S(1)} %get-tuple-element.37.parts_ref, f32[96,256]{1,0:T(8,128)S(1)} %get-tuple-element.38.cond_ref, s32[1,512]{1,0:T(1,128)S(1)} %bitcast.6), custom_call_target="tpu_custom_call" | custom-call | flops 5000000000 | bytes 1000000 | tf_op jit(solution)/shard_map/ionosphere/pallas_call | solution.py:381
  85.4 0.0 collective-permute-done.4.lower_ref
  85.4 7.7 %step.7 = f32[8,8,8,8,512]{4,3,2,1,0:T(8,128)} custom-call(s32[1]{0:T(128)} %bitcast.base_ref, s32[1]{0:T(128)S(6)} %copy.10.count_ref, f32[8]{0:T(128)S(1)} %copy-done.4, s32[6,512]{1,0:T(8,128)S(1)} %copy-done.1, f32[4,40,8,128]{3,2,1,0:T(8,128)S(1)} %collective-permute-done.4.lower_ref, ...), custom_call_target="tpu_custom_call", output_to_operand_aliasing={{}: (8, {})} | custom-call | flops 5000000000 | bytes 30000000 | tf_op jit(solution)/shard_map/step/pallas_call | solution.py:323
  (12 shorter events, 0.0 us)
Async XLA Ops:
  1.3 27.7 %copy-start.1 = (s32[6,512]{1,0:T(8,128)S(1)}, s32[6,512]{1,0:T(8,128)}, u32[]{:S(2)}) copy-start(s32[6,512]{1,0:T(8,128)} %near_ref.7) | copy-start | bytes 36868
  1.3 27.7 %copy-start.4 = (f32[8]{0:T(128)S(1)}, f32[8]{0:T(128)}, u32[]{:S(2)}) copy-start(f32[8]{0:T(128)} %rates_ref.7) | copy-start | bytes 100
  3.8 7.1 %collective-permute-start = (f32[4,40,8,128]{3,2,1,0:T(8,128)S(1)}, f32[4,40,8,128]{3,2,1,0:T(8,128)S(1)}, u32[]{:S(2)}, u32[]{:S(2)}) collective-permute-start(f32[4,40,8,128]{3,2,1,0:T(8,128)S(1)} %get-tuple-element.25), channel_id=1, source_target_pairs={{0,1},{1,2},{2,3},{3,4},{4,5},{5,6},{6,7},{7,8},{8,9},{9,10},{10,1... | collective-permute-start | bytes 1966088 | tf_op jit(solution)/shard_map/ppermute | solution.py:308
  6.2 6.1 %collective-permute-start.1 = (f32[4,40,8,128]{3,2,1,0:T(8,128)S(1)}, f32[4,40,8,128]{3,2,1,0:T(8,128)S(1)}, u32[]{:S(2)}, u32[]{:S(2)}) collective-permute-start(f32[4,40,8,128]{3,2,1,0:T(8,128)S(1)} %get-tuple-element.22.refs_0_), channel_id=1, source_target_pairs={{1,0},{2,1},{3,2},{4,3},{5,4},{6,5},{7,6},{8,7},{9,8},{10,9},{11,1... | collective-permute-start | bytes 1966088 | tf_op jit(solution)/shard_map/ppermute | solution.py:308
  12.3 30.2 %collective-permute-start.2 = (f32[4,40,8,128]{3,2,1,0:T(8,128)}, f32[4,40,8,128]{3,2,1,0:T(8,128)}, u32[]{:S(2)}, u32[]{:S(2)}) collective-permute-start(f32[4,40,8,128]{3,2,1,0:T(8,128)} %get-tuple-element.26), channel_id=1, source_target_pairs={{0,1},{1,2},{2,3},{3,4},{4,5},{5,6},{6,7},{7,8},{8,9},{9,10},{10,1... | collective-permute-start | bytes 1966088 | tf_op jit(solution)/shard_map/ppermute | solution.py:308
  27.7 14.7 %collective-permute-start.3 = (f32[4,40,8,128]{3,2,1,0:T(8,128)S(1)}, f32[4,40,8,128]{3,2,1,0:T(8,128)}, u32[]{:S(2)}, u32[]{:S(2)}) collective-permute-start(f32[4,40,8,128]{3,2,1,0:T(8,128)S(1)} %get-tuple-element.27), channel_id=1, source_target_pairs={{1,0},{2,1},{3,2},{4,3},{5,4},{6,5},{7,6},{8,7},{9,8},{10,9},{11,1... | collective-permute-start | bytes 1966088 | tf_op jit(solution)/shard_map/ppermute | solution.py:308
  38.1 19.0 %collective-permute-start.6 = (f32[4,40,8,128]{3,2,1,0:T(8,128)}, f32[4,40,8,128]{3,2,1,0:T(8,128)S(1)}, u32[]{:S(2)}, u32[]{:S(2)}) collective-permute-start(f32[4,40,8,128]{3,2,1,0:T(8,128)} %get-tuple-element.34), channel_id=1, source_target_pairs={{0,1},{1,2},{2,3},{3,4},{4,5},{5,6},{6,7},{7,8},{8,9},{9,10},{10,1... | collective-permute-start | bytes 1966088 | tf_op jit(solution)/shard_map/ppermute | solution.py:308
  41.1 15.9 %collective-permute-start.7 = (f32[4,40,8,128]{3,2,1,0:T(8,128)S(1)}, f32[4,40,8,128]{3,2,1,0:T(8,128)S(1)}, u32[]{:S(2)}, u32[]{:S(2)}) collective-permute-start(f32[4,40,8,128]{3,2,1,0:T(8,128)S(1)} %get-tuple-element.30.refs_0_), channel_id=1, source_target_pairs={{1,0},{2,1},{3,2},{4,3},{5,4},{6,5},{7,6},{8,7},{9,8},{10,9},{11,1... | collective-permute-start | bytes 1966088 | tf_op jit(solution)/shard_map/ppermute | solution.py:308
  42.4 14.6 %copy-start.5 = (f32[4,8,8,8,512]{4,3,2,1,0:T(8,128)S(1)}, f32[4,8,8,8,512]{4,3,2,1,0:T(8,128)}, u32[]{:S(2)}) copy-start(f32[4,8,8,8,512]{4,3,2,1,0:T(8,128)} %get-tuple-element.35.u_ref) | copy-start | bytes 12582916
  51.8 33.6 %collective-permute-start.4 = (f32[4,40,8,128]{3,2,1,0:T(8,128)S(1)}, f32[4,40,8,128]{3,2,1,0:T(8,128)S(1)}, u32[]{:S(2)}, u32[]{:S(2)}) collective-permute-start(f32[4,40,8,128]{3,2,1,0:T(8,128)S(1)} %get-tuple-element.31), channel_id=1, source_target_pairs={{0,1},{1,2},{2,3},{3,4},{4,5},{5,6},{6,7},{7,8},{8,9},{9,10},{10,1... | collective-permute-start | bytes 1966088 | tf_op jit(solution)/shard_map/ppermute | solution.py:308
  55.6 29.8 %collective-permute-start.5 = (f32[4,40,8,128]{3,2,1,0:T(8,128)S(1)}, f32[4,40,8,128]{3,2,1,0:T(8,128)S(1)}, u32[]{:S(2)}, u32[]{:S(2)}) collective-permute-start(f32[4,40,8,128]{3,2,1,0:T(8,128)S(1)} %get-tuple-element.32.refs_0_), channel_id=1, source_target_pairs={{1,0},{2,1},{3,2},{4,3},{5,4},{6,5},{7,6},{8,7},{9,8},{10,9},{11,1... | collective-permute-start | bytes 1966088 | tf_op jit(solution)/shard_map/ppermute | solution.py:308
  57.1 7.3 %copy-start.2 = (f32[12,256]{1,0:T(8,128)S(1)}, f32[12,256]{1,0:T(8,128)}, u32[]{:S(2)}) copy-start(f32[12,256]{1,0:T(8,128)} %cond_ref.1) | copy-start | bytes 36868
  57.1 7.3 %copy-start.3 = (s32[512]{0:T(512)S(1)}, s32[512]{0:T(512)}, u32[]{:S(2)}) copy-start(s32[512]{0:T(512)} %param.9) | copy-start | bytes 6148
  79.3 6.1 %copy-start = (f32[4,8,8,8,512]{4,3,2,1,0:T(8,128)S(1)}, f32[4,8,8,8,512]{4,3,2,1,0:T(8,128)}, u32[]{:S(2)}) copy-start(f32[4,8,8,8,512]{4,3,2,1,0:T(8,128)} %get-tuple-element.33.u_ref) | copy-start | bytes 12582916
